TPU v7x, 512 devices: a whole 4x4x16 slice. The times are simulated.
512 devices in a mesh: group: 16 (over x_lo, y, core), shard: 32 (over x_hi, z).
Axes of the slice: x: 4 (x_hi: 2, x_lo: 2; x = x_hi * 2 + x_lo), y: 4, z: 16, core: 2. Of those that a mesh axis runs over, the one named last changes fastest.
Arguments:
- patches: bfloat16 [3, 1024, 5120], P(None, ('group', 'shard')), may hold values from -24 to 24
- image_lengths: int32 [3, 4], replicated, may hold values from 1 to 512, 1024 in all within a row
- destination: int32 [3, 16], replicated, may hold values from 0 to 15, each once within a row
- query_key_value_weight: bfloat16 [5120, 32, 384], P('group', 'shard'), may hold values from -0.078125 to 0.078125
Outputs:
- attended: bfloat16 [3, 1024, 32, 128], P(None, 'group', 'shard')
All inputs are finite; a program needn't handle non-finite values.
Results may differ from a plain program's by a relative error of at most 0.012.
The roundings to bfloat16 on the way count: a program that leaves them out, or rounds other values in their place, can miss the bound.
Values may be sent and summed in bfloat16 or wider, within the bound.
No kernel may reach another device: no remote copies, remote signals or barrier semaphores. Data moves between devices by JAX's collectives and lax.ppermute only.
A program may use at most 64 MiB of HBM per device.

v0:
```python
import jax
import jax.numpy as jnp
from jax import lax
from jax.sharding import PartitionSpec as P

HD = 128


def attend(query_matrix, projected_key_rows, projected_value_rows, query_ids, key_ids):
    score_scale = HD ** (-0.5)
    scores = (
        jnp.einsum(
            "auh,afh->auf", query_matrix, projected_key_rows, preferred_element_type=jnp.float32
        )
        * score_scale
    )
    same_image = query_ids[:, :, None] == key_ids[:, None, :]
    scores = jnp.where(same_image, scores, -jnp.inf)
    row_max = jnp.max(scores, axis=-1, keepdims=True)
    attention_probabilities = jnp.exp(scores - row_max)
    attention_probabilities = (
        attention_probabilities / jnp.sum(attention_probabilities, axis=-1, keepdims=True)
    ).astype(jnp.bfloat16)
    attention_output = jnp.einsum(
        "mal,mlu->mau",
        attention_probabilities,
        projected_value_rows,
        preferred_element_type=jnp.float32,
    )
    return attention_output.astype(jnp.bfloat16)


def shards(patches, image_lengths, destination, query_key_value_weight):
    groups = lax.axis_size("group")
    group_index = lax.axis_index("group")
    npacks = patches.shape[0]
    complete_weight_matrix = lax.all_gather(query_key_value_weight, "group", axis=0, tiled=True)
    weight_mat = complete_weight_matrix.reshape(
        complete_weight_matrix.shape[0],
        complete_weight_matrix.shape[1] * complete_weight_matrix.shape[2],
    )
    group_ids = jnp.arange(groups, dtype=jnp.int32)
    own_dest = lax.dynamic_slice_in_dim(destination, group_index, 1, 1)[:, 0]
    to_group = (own_dest[None, :] == group_ids[:, None]).astype(jnp.bfloat16)
    from_group = (destination == group_index).astype(jnp.bfloat16)
    outgoing = to_group[:, :, None, None] * patches[None]
    arrived = lax.all_to_all(outgoing, "group", split_axis=0, concat_axis=0, tiled=True)
    local_rows = jnp.einsum(
        "pg,gprd->prd", from_group, arrived, preferred_element_type=jnp.float32
    ).astype(jnp.bfloat16)
    proj = jnp.einsum(
        "prd,dc->prc",
        lax.all_gather(local_rows, "shard", axis=1, tiled=True),
        weight_mat,
        preferred_element_type=jnp.float32,
    ).astype(jnp.bfloat16)
    block_len = proj.shape[1]
    query_matrix = proj[:, :, 0:HD]
    projected_key_rows = proj[:, :, HD : 2 * HD]
    projected_value_rows = proj[:, :, 2 * HD : 3 * HD]
    whole_keys, whole_values = (
        lax.all_gather(projected_key_rows, "group", axis=1, tiled=True),
        lax.all_gather(projected_value_rows, "group", axis=1, tiled=True),
    )
    pack_len = whole_keys.shape[1]
    positions = jnp.arange(pack_len, dtype=jnp.int32)
    image_ends = jnp.cumsum(image_lengths, axis=-1)
    segment = jnp.sum(
        (positions[None, :, None] >= image_ends[:, None, :]).astype(jnp.int32), axis=-1
    )
    query_ids = lax.dynamic_slice_in_dim(segment, group_index * block_len, block_len, 1)
    pack_slots = jnp.arange(npacks, dtype=jnp.int32)[:, None] * (image_lengths.shape[1] + 2)
    attention_output = attend(
        query_matrix.reshape(1, npacks * block_len, HD),
        whole_keys.reshape(1, npacks * pack_len, HD),
        whole_values.reshape(1, npacks * pack_len, HD),
        (pack_slots + query_ids).reshape(1, npacks * block_len),
        (pack_slots + segment).reshape(1, npacks * pack_len),
    )
    attention_output = attention_output.reshape(npacks, block_len, HD)
    return attention_output.reshape(npacks, block_len, 1, HD)


def solution(mesh):
    placed = (P(None, ("group", "shard"), None), P(), P(), P("group", "shard", None))
    return jax.shard_map(
        shards,
        mesh=mesh,
        in_specs=placed,
        out_specs=P(None, "group", "shard", None),
        check_vma=False,
    )
```

profile of v0, /device:TPU:1, one launch (start us, length us, event | category | flops | bytes accessed | tf_op | source)
XLA Modules:
  0.0 283.6 jit_solution(10302997126400528146)
XLA Ops:
  6.5 0.9 dynamic-slice_reduce_fusion
  7.5 2.6 broadcast_multiply_fusion
  10.0 10.3 %all-to-all-start = ((bf16[16,3,2,5120]{3,2,1,0:T(2,128)(2,1)}), bf16[16,3,2,5120]{3,2,1,0:T(2,128)(2,1)S(1)}, u32[]{:S(2)}, u32[]{:S(2)}) async-start(bf16[16,3,2,5120]{3,2,1,0:T(2,128)(2,1)} %broadcast_multiply_fusion), calls=%async_computation | async-start | bytes 1966080 | tf_op jit(solution)/shard_map/all_to_all | solution.py:47
  20.4 0.0 all-gather.3.cloned.1.call-start
  20.4 0.0 copy-done
  20.4 15.1 %all-to-all-done = bf16[16,3,2,5120]{3,2,1,0:T(2,128)(2,1)S(1)} async-done(((bf16[16,3,2,5120]{3,2,1,0:T(2,128)(2,1)}), bf16[16,3,2,5120]{3,2,1,0:T(2,128)(2,1)S(1)}, u32[]{:S(2)}, u32[]{:S(2)}) %all-to-all-start) | async-done | bytes 983072 | tf_op jit(solution)/shard_map/all_to_all | solution.py:47
  35.5 0.3 fusion.12
  35.8 0.7 copy.22
  36.5 0.0 all-gather.3.cloned.1.call-update
  36.6 0.0 all-gather.5.cloned.1.call-start
  36.6 0.7 all-gather.5.cloned.1.call-update
  37.3 0.2 reduce_window_sum.11
  37.5 0.1 convert_reduce_fusion
  37.6 0.1 broadcast_add_fusion
  37.7 0.1 dynamic-slice_add_fusion
  37.8 0.1 eq.41
  37.9 142.4 %all-gather.3.cloned.1.call-done = bf16[3,64,5120]{2,0,1:T(4,128)(2,1)} async-done(((bf16[3,2,5120]{2,0,1:T(4,128)(2,1)}), bf16[3,64,5120]{2,0,1:T(4,128)(2,1)}) %all-gather.3.cloned.1.call-update) | async-done | bytes 1966096 | tf_op jit(solution)/shard_map/all_gather | solution.py:53
  180.3 51.2 %all-gather.5.cloned.1.call-done = bf16[5120,1,384]{2,0,1:T(8,128)(2,1)} async-done(((bf16[320,1,384]{2,0,1:T(8,128)(2,1)}), bf16[5120,1,384]{2,0,1:T(8,128)(2,1)}) %all-gather.5.cloned.1.call-update) | async-done | bytes 3932176 | tf_op jit(solution)/shard_map/all_gather | solution.py:37
  231.5 4.2 %fusion.6 = bf16[3,64,384]{2,1,0:T(8,128)(2,1)S(1)} fusion(bf16[5120,1,384]{2,0,1:T(8,128)(2,1)} %all-gather.5.cloned.1.call-done, bf16[3,64,5120]{2,0,1:T(4,128)(2,1)} %all-gather.3.cloned.1.call-done), kind=kOutput, calls=%fused_computation.9 | convolution fusion | flops 755048448 | bytes 6045696 | tf_op jit(solution)/shard_map/prd,dc->prc/dot_general | solution.py:51
  235.7 20.2 %all_gather.15 = bf16[3,1024,128]{2,1,0:T(8,128)(2,1)S(1)} all-gather(bf16[3,64,128]{2,1,0:T(8,128)(2,1)S(1)} %get-tuple-element.6), channel_id=1, replica_groups=mesh['group'=16,'shard'=32] {'group'}, dimensions={1}, use_global_device_ids=true | all-gather | bytes 835584 | tf_op jit(solution)/shard_map/all_gather | solution.py:63
  255.9 18.4 %all_gather.14 = bf16[3,1024,128]{2,1,0:T(8,128)(2,1)S(1)} all-gather(bf16[3,64,128]{2,1,0:T(8,128)(2,1)S(1)} %get-tuple-element.5), channel_id=1, replica_groups=mesh['group'=16,'shard'=32] {'group'}, dimensions={1}, use_global_device_ids=true | all-gather | bytes 835584 | tf_op jit(solution)/shard_map/all_gather | solution.py:62
  274.4 0.6 fusion.17
  274.9 0.5 fusion.3
  275.4 1.3 fusion.11
  (8 shorter events, 0.1 us)
Async XLA Ops:
  6.5 13.9 %copy-start = (s32[3,16]{1,0:T(4,128)S(1)}, s32[3,16]{1,0:T(4,128)}, u32[]{:S(2)}) copy-start(s32[3,16]{1,0:T(4,128)} %param.6) | copy-start | bytes 580
  6.5 30.8 %copy-start.1 = (s32[3,4]{1,0:T(4,128)S(1)}, s32[3,4]{1,0:T(4,128)}, u32[]{:S(2)}) copy-start(s32[3,4]{1,0:T(4,128)} %param.5) | copy-start | bytes 148
  10.0 25.5 %all-to-all-start = ((bf16[16,3,2,5120]{3,2,1,0:T(2,128)(2,1)}), bf16[16,3,2,5120]{3,2,1,0:T(2,128)(2,1)S(1)}, u32[]{:S(2)}, u32[]{:S(2)}) async-start(bf16[16,3,2,5120]{3,2,1,0:T(2,128)(2,1)} %broadcast_multiply_fusion), calls=%async_computation | async-start | bytes 1966080 | tf_op jit(solution)/shard_map/all_to_all | solution.py:47
  20.4 159.9 %all-gather.3.cloned.1.call-start = ((), (), s32[]{:S(2)}) async-start(), calls=%async_computation.1 | async-start | bytes 2703360 | tf_op jit(solution)/shard_map/all_gather | solution.py:53
  36.6 194.9 %all-gather.5.cloned.1.call-start = ((), (), s32[]{:S(2)}) async-start(), calls=%async_computation.2 | async-start | bytes 4177920 | tf_op jit(solution)/shard_map/all_gather | solution.py:37
Sparse Core Ops, SparseCore 0:
  36.7 143.5 all-gather.2
  182.4 49.0 all-gather.4
where the time goes:
time: 284 us
  waiting for transfers between devices  209 us (74%)
  blocking collectives  38.6 us (14%)
  between operations  13.5 us (5%)
  starting transfers between devices  10.4 us (4%)
  matrix products  6.39 us (2%)
  other arithmetic  3.5 us (1%)
    all_gather x1, waiting for transfers between devices, shards(): lax.all_gather(local_rows, 'shard', axis=1, tiled=True)  142 us
    all_gather x1, waiting for transfers between devices, shards(): lax.all_gather(query_key_value_weight, 'group', axis=0, tiled=True)  51.2 us
    all_gather x1, blocking collectives, shards(): lax.all_gather(projected_value_rows, 'group', axis=1, tiled=True)  20.2 us
    all_gather x1, blocking collectives, shards(): lax.all_gather(projected_key_rows, 'group', axis=1, tiled=True)  18.4 us
    all_to_all x1, waiting for transfers between devices, shards(): lax.all_to_all(outgoing, 'group', split_axis=0, concat_axis=0, tiled=True)  15.1 us
    all_to_all x1, starting transfers between devices, shards(): lax.all_to_all(outgoing, 'group', split_axis=0, concat_axis=0, tiled=True)  10.3 us
  transfers between devices with their start and end apart: 3, of which 3 were waited for; matrix products, arithmetic and copies ran while one was open for 0% of the time, Pallas kernels for 0%

commit v1 on v0

v1 whole, which is shorter than its diff:
```python
import jax
import jax.numpy as jnp
from jax import lax
from jax.experimental import pallas as pl
from jax.experimental.pallas import tpu as pltpu
from jax.sharding import Mesh, PartitionSpec as P

D = 5120
HD = 128
BLK = 64
HALF = BLK // 2
NPACK = 3
IMGS = 4
NBLK = 16
QKV = 3 * HD
SENT = 5 * HD
NZ = 16
PIECE = D // 16
KSET = 4 * PIECE
LOCAL = NPACK * 2
ROWS = NPACK * BLK

FINE = (("xl", 2), ("y", 4), ("c", 2), ("xh", 2), ("z", 16))
GROUP = ("xl", "y", "c")
SHARD = ("xh", "z")
PACK_OF = (0, 1, 2, 2)
VMEM_BYTES = 32 * 2**20


def spread_kernel(w_ref, out_ref, sems):
    copies = [pltpu.make_async_copy(w_ref, out_ref.at[m], sems.at[m]) for m in range(8)]
    for copy in copies:
        copy.start()
    for copy in copies:
        copy.wait()


def column_kernel(x_ref, out_ref):
    own_xl, own_c = lax.axis_index("xl") == 1, lax.axis_index("c") == 1
    x = x_ref[...].astype(jnp.float32)
    x = jnp.where(own_xl, x[..., D // 2 :], x[..., : D // 2])
    x = jnp.concatenate([x[k, p] for k in range(4) for p in range(NPACK)], axis=0)
    cut = [
        jnp.where(own_c, x[:, (2 * y + 1) * PIECE : (2 * y + 2) * PIECE], x[:, 2 * y * PIECE : (2 * y + 1) * PIECE])
        for y in range(4)
    ]
    out_ref[...] = jnp.concatenate(cut, axis=1).astype(jnp.bfloat16)


def split(product):
    whole_part = product.astype(jnp.bfloat16)
    scored = slice(0, 2 * HD)
    rest = (product[:, scored] - whole_part[:, scored].astype(jnp.float32)).astype(jnp.bfloat16)
    return whole_part, rest


def joined(sent):
    scored = sent[:, : 2 * HD].astype(jnp.float32) + sent[:, QKV:].astype(jnp.float32)
    return scored, sent[:, 2 * HD : QKV].astype(jnp.float32)


def project_kernel(x_ref, w_ref, keep_ref, give_ref, product_ref):
    own = lax.axis_index("c")
    for head in range(2):
        product = jnp.dot(
            x_ref[...], w_ref[:, head].reshape(KSET, QKV), preferred_element_type=jnp.float32
        )
        for k in range(3):
            product_ref[k] = product[:, k * HD : (k + 1) * HD]
            columns = slice(head * QKV + k * HD, head * QKV + (k + 1) * HD)
            sent = slice(head * SENT + k * HD, head * SENT + (k + 1) * HD)
            remainder = slice(head * SENT + QKV + k * HD, head * SENT + QKV + (k + 1) * HD)
            for p in range(NPACK):
                for xl in range(2):
                    for i in range(2):
                        at = p * BLK + xl * HALF + i * NZ
                        first = xl * 2 * LOCAL + p * 2 + i
                        mine = product_ref[k, pl.ds(first + own * LOCAL, NZ, stride=4 * LOCAL), :]
                        theirs = product_ref[k, pl.ds(first + (1 - own) * LOCAL, NZ, stride=4 * LOCAL), :]
                        keep_ref[at : at + NZ, columns] = mine
                        rounded = theirs.astype(jnp.bfloat16)
                        give_ref[at : at + NZ, sent] = rounded
                        if k < 2:
                            rest = theirs - rounded.astype(jnp.float32)
                            give_ref[at : at + NZ, remainder] = rest.astype(jnp.bfloat16)


def pair_kernel(keep_ref, got_ref, out_ref):
    other = 1 - lax.axis_index("c")
    for p in range(NPACK):
        rows = slice(p * BLK, (p + 1) * BLK)
        for head in range(2):
            scored, value = joined(got_ref[other, rows, head * SENT : (head + 1) * SENT])
            total = keep_ref[rows, head * QKV : (head + 1) * QKV]
            total = jnp.concatenate([total[:, : 2 * HD] + scored, total[:, 2 * HD :] + value], axis=1)
            rounded, rest = split(total)
            for y, pack in enumerate(PACK_OF):
                if pack == p:
                    for xl in range(2):
                        out_ref[xl * 8 + y * 2 + head, :, :QKV] = rounded
                        out_ref[xl * 8 + y * 2 + head, :, QKV:] = rest


def total_kernel(parts_ref, out_ref):
    for y in range(4):
        for xh in range(2):
            at = y * 2 + xh
            scored, value = joined(parts_ref[at])
            more_scored, more_value = joined(parts_ref[8 + at])
            scored = (scored + more_scored).astype(jnp.bfloat16)
            value = (value + more_value).astype(jnp.bfloat16)
            for xl in range(2):
                block, half = slice(xl * HALF, (xl + 1) * HALF), slice(xh * HALF, (xh + 1) * HALF)
                out_ref[xl * 4 + y, half, : 2 * HD] = scored[block]
                out_ref[xl * 4 + y, half, 2 * HD :] = value[block]


def row_of(at):
    return (at & HALF) + ((at & (NZ - 1)) << 1) + ((at >> 4) & 1)


def attend_kernel(destination_ref, lengths_ref, qkv_ref, out_ref, ordered_ref):
    xl, y_own, c = (lax.axis_index(a) for a in ("xl", "y", "c"))
    pack = jnp.minimum(y_own, NPACK - 1)
    ends = []
    end = 0
    for i in range(IMGS):
        end = end + lengths_ref[pack, i]
        ends.append(end)

    def segment(position):
        count = jnp.zeros(position.shape, jnp.int32)
        for e in ends:
            count = count + (position >= e).astype(jnp.int32)
        return count

    lane = lax.broadcasted_iota(jnp.int32, (1, NBLK * BLK), 1)
    key_block = jnp.zeros_like(lane)
    slots = []
    for j in range(NBLK):
        slot = (j & 1) * 8 + (j >> 1)
        slots.append(slot)
        key_block = jnp.where((lane >> 6) == slot, destination_ref[pack, j], key_block)
    key_ids = segment(key_block * BLK + row_of(lane))

    queries = []
    for y in range(4):
        block = xl * 8 + y * 2 + c
        start = 0
        for j in range(NBLK):
            start = jnp.where(destination_ref[pack, j] == block, slots[j] * BLK, start)
        start = pl.multiple_of(start, BLK)
        queries.append(qkv_ref[pl.ds(start, BLK), 0:HD])
    query = jnp.concatenate(queries, axis=0)
    row = lax.broadcasted_iota(jnp.int32, (4 * BLK, 1), 0)
    query_ids = segment((xl * 8 + c) * BLK + (row >> 6) * (2 * BLK) + row_of(row))

    scores = lax.dot_general(
        query,
        qkv_ref[:, HD : 2 * HD],
        (((1,), (1,)), ((), ())),
        preferred_element_type=jnp.float32,
    ) * (HD**-0.5)
    scores = jnp.where(query_ids == key_ids, scores, -jnp.inf)
    weights = jnp.exp(scores - jnp.max(scores, axis=-1, keepdims=True))
    weights = (weights * (1.0 / jnp.sum(weights, axis=-1, keepdims=True))).astype(jnp.bfloat16)
    attended = jnp.dot(weights, qkv_ref[:, 2 * HD : 3 * HD], preferred_element_type=jnp.float32)
    for at in range(0, 4 * BLK, NZ):
        first = at // HALF * HALF + (at // NZ) % 2
        ordered_ref[pl.ds(first, NZ, stride=2), :] = attended[at : at + NZ]
    for y in range(4):
        out_ref[y] = ordered_ref[y * BLK : (y + 1) * BLK].astype(jnp.bfloat16)


def whole(memory=pltpu.VMEM):
    return pl.BlockSpec(memory_space=memory)


def call(kernel, out, in_specs, scratch=(), cost=(0, 10**6, 0), out_specs=None):
    flops, bytes_accessed, transcendentals = cost
    return pl.pallas_call(
        kernel,
        out_shape=out,
        in_specs=in_specs,
        out_specs=out_specs or jax.tree.map(lambda _: whole(), out),
        scratch_shapes=list(scratch),
        compiler_params=pltpu.CompilerParams(vmem_limit_bytes=VMEM_BYTES),
        cost_estimate=pl.CostEstimate(
            flops=flops, bytes_accessed=bytes_accessed, transcendentals=transcendentals
        ),
    )


def shards(patches, image_lengths, destination, weight):
    half_type = jnp.bfloat16

    slots = call(
        spread_kernel,
        jax.ShapeDtypeStruct((8, PIECE, QKV), half_type),
        [whole(pl.ANY)],
        [pltpu.SemaphoreType.DMA((8,))],
        out_specs=whole(pl.ANY),
    )(weight.reshape(PIECE, QKV))
    near = lax.all_gather(patches, ("xl", "c"), axis=0)
    slots, near = lax.optimization_barrier((slots, near))
    weight_set = lax.all_to_all(slots, ("y", "xh"), 0, 0, tiled=True)

    rows = call(
        column_kernel, jax.ShapeDtypeStruct((4 * LOCAL, KSET), half_type), [whole()]
    )(near)
    rows = lax.all_gather(rows, "z", axis=0, tiled=True)

    keep, give = call(
        project_kernel,
        (
            jax.ShapeDtypeStruct((ROWS, 2 * QKV), jnp.float32),
            jax.ShapeDtypeStruct((ROWS, 2 * SENT), half_type),
        ),
        [whole(), whole()],
        [pltpu.VMEM((3, 4 * LOCAL * NZ, HD), jnp.float32)],
        cost=(10**9, 4 * 10**6, 0),
    )(rows, weight_set.reshape(4, 2, PIECE, QKV))

    got = lax.all_gather(give, "c", axis=0)
    spread = call(
        pair_kernel,
        jax.ShapeDtypeStruct((16, BLK, SENT), half_type),
        [whole(), whole()],
    )(keep, got)
    parts = lax.all_to_all(spread, ("xl", "y", "xh"), 0, 0, tiled=True)
    blocks = call(total_kernel, jax.ShapeDtypeStruct((8, BLK, QKV), half_type), [whole()])(parts)
    blocks = lax.all_gather(blocks.reshape(8 * BLK, QKV), "c", axis=0, tiled=True)

    attended = call(
        attend_kernel,
        jax.ShapeDtypeStruct((4, BLK, HD), half_type),
        [whole(pltpu.SMEM)] * 2 + [whole()],
        [pltpu.VMEM((4 * BLK, HD), jnp.float32)],
        cost=(2 * 10**8, 10**6, 3 * 10**5),
    )(destination, image_lengths, blocks)

    home = lax.all_to_all(attended, "y", 0, 0, tiled=True)
    return home[:NPACK].reshape(NPACK, BLK, 1, HD)


def solution(mesh):
    names, sizes = zip(*FINE)
    fine = Mesh(mesh.devices.reshape(sizes), names)
    return jax.shard_map(
        shards,
        mesh=fine,
        in_specs=(P(None, GROUP + SHARD, None), P(), P(), P(GROUP, SHARD, None)),
        out_specs=P(None, GROUP, SHARD, None),
        check_vma=False,
    )
```

time: 284 us -> 101 us (0.36)
  waiting for transfers between devices: 209 us -> 0.01 us
  blocking collectives: 38.6 us -> 90.8 us
  between operations: 13.5 us -> 0.04 us
  starting transfers between devices: 10.4 us -> 3.61 us
  matrix products: 6.39 us -> 0 us
  Pallas kernels: 0 us -> 4.72 us
  other arithmetic: 3.5 us -> 0 us
    all_gather x2 -> x0, waiting for transfers between devices: 194 us -> none  [the longest x1 142 us: shards(): lax.all_gather(local_rows, 'shard', axis=1, tiled=True)]
    all_to_all x0 -> x2, blocking collectives: none -> 32.4 us  [the longest x1 25.6 us: shards(): parts = lax.all_to_all(spread, ('xl', 'y', 'xh'), 0, 0, tiled=True)]
    all_gather x2 -> x4, blocking collectives: 38.6 us -> 58.3 us  [the longest x1 34.3 us: shards(): rows = lax.all_gather(rows, 'z', axis=0, tiled=True)]
    all_to_all x1, waiting for transfers between devices: 15.1 us -> 0.01 us  [shards(): weight_set = lax.all_to_all(slots, ('y', 'xh'), 0, 0, tiled=True)]
    all_to_all x1, starting transfers between devices: 10.3 us -> 3.61 us  [shards(): weight_set = lax.all_to_all(slots, ('y', 'xh'), 0, 0, tiled=True)]
    dot_general x4 -> x0, matrix products: 6.39 us -> none  [the longest x1 4.21 us: shards(): jnp.einsum('prd,dc->prc', lax.all_gather(local_rows, 'shard', axis=1, til...]
    pallas_call x0 -> x6, Pallas kernels: none -> 4.72 us  [the longest x1 1.45 us: shards(): call(attend_kernel, jax.ShapeDtypeStruct((4, BLK, HD), half_type), [whole...]
  transfers between devices with their start and end apart: 3 -> 1, of which waited for: 3 -> 0; matrix products, arithmetic and copies ran while one was open for 0% -> 0% of each run, Pallas kernels for 0% -> 0%
where the time goes in v1:
time: 101 us
  blocking collectives  90.8 us (90%)
  Pallas kernels  4.72 us (5%)
  starting transfers between devices  3.61 us (4%)
  local copies, waits for them, and re-layouts  1.58 us (2%)
    all_gather x1, blocking collectives, shards(): rows = lax.all_gather(rows, 'z', axis=0, tiled=True)  34.3 us
    all_to_all x1, blocking collectives, shards(): parts = lax.all_to_all(spread, ('xl', 'y', 'xh'), 0, 0, tiled=True)  25.6 us
    all_gather x1, blocking collectives, shards(): near = lax.all_gather(patches, ('xl', 'c'), axis=0)  12.7 us
    all_gather x1, blocking collectives, shards(): got = lax.all_gather(give, 'c', axis=0)  7.41 us
    all_to_all x1, blocking collectives, shards(): home = lax.all_to_all(attended, 'y', 0, 0, tiled=True)  6.84 us
    all_gather x1, blocking collectives, shards(): lax.all_gather(blocks.reshape(8 * BLK, QKV), 'c', axis=0, tiled=True)  4 us
    all_to_all x1, starting transfers between devices, shards(): weight_set = lax.all_to_all(slots, ('y', 'xh'), 0, 0, tiled=True)  3.61 us
  transfers between devices with their start and end apart: 1, of which 0 were waited for; matrix products, arithmetic and copies ran while one was open for 0% of the time, Pallas kernels for 0%

profile of v1, /device:TPU:1, one launch (start us, length us, event | category | flops | bytes accessed | tf_op | source)
XLA Modules:
  0.0 100.7 jit_solution(7561460642628240474)
XLA Ops:
  0.0 12.7 %all-gather = bf16[12,2,5120]{2,1,0:T(2,128)(2,1)S(1)} all-gather(bf16[3,2,5120]{2,1,0:T(2,128)(2,1)} %param.4), channel_id=2, replica_groups=mesh['xl'=2,'y'=4,'c'=2,'xh'=2,'z'=16] {'xl','c'}, dimensions={0}, use_global_device_ids=true | all-gather | bytes 307200 | tf_op jit(solution)/shard_map/all_gather | solution.py:204
  12.7 0.0 copy-start
  12.7 0.9 copy-done
  13.6 1.4 %shard_map.46 = bf16[8,320,384]{2,1,0:T(8,128)(2,1)} custom-call(bf16[320,384]{1,0:T(8,128)(2,1)S(1)} %bitcast.13), custom_call_target="tpu_custom_call" | custom-call | bytes 1000000 | tf_op jit(solution)/shard_map/pallas_call | solution.py:197
  15.0 3.6 %all-to-all-start = ((bf16[8,320,384]{2,1,0:T(8,128)(2,1)}), bf16[8,320,384]{2,1,0:T(8,128)(2,1)S(1)}, u32[]{:S(2)}, u32[]{:S(2)}) async-start(bf16[8,320,384]{2,1,0:T(8,128)(2,1)} %shard_map.46), calls=%async_computation | async-start | bytes 3932160 | tf_op jit(solution)/shard_map/all_to_all | solution.py:206
  18.6 0.2 shard_map.47
  18.8 34.3 %all_gather.20.x_ref = bf16[384,1280]{1,0:T(8,128)(2,1)S(1)} all-gather(bf16[24,1280]{1,0:T(8,128)(2,1)S(1)} %shard_map.47), channel_id=1, replica_groups=mesh['xl'=2,'y'=4,'c'=2,'xh'=2,'z'=16] {'z'}, dimensions={0}, use_global_device_ids=true | all-gather | bytes 1044480 | tf_op jit(solution)/shard_map/all_gather | solution.py:211
  53.1 0.0 all-to-all-done
  53.1 1.3 %shard_map.48 = (f32[192,768]{1,0:T(8,128)S(1)}, bf16[192,1280]{1,0:T(8,128)(2,1)S(1)}) custom-call(bf16[384,1280]{1,0:T(8,128)(2,1)S(1)} %all_gather.20.x_ref, bf16[4,2,320,384]{3,2,1,0:T(8,128)(2,1)S(1)} %bitcast.10), custom_call_target="tpu_custom_call" | custom-call | flops 1000000000 | bytes 4000000 | tf_op jit(solution)/shard_map/pallas_call | solution.py:213
  54.4 7.4 %all-gather.1 = bf16[384,1280]{1,0:T(8,128)(2,1)S(1)} all-gather(bf16[192,1280]{1,0:T(8,128)(2,1)S(1)} %get-tuple-element.12), channel_id=3, replica_groups=mesh['xl'=2,'y'=4,'c'=2,'xh'=2,'z'=16] {'c'}, dimensions={0}, use_global_device_ids=true | all-gather | bytes 1474560 | tf_op jit(solution)/shard_map/all_gather | solution.py:224
  61.8 0.1 shard_map.49
  62.0 25.6 %all_to_all.15.parts_ref = bf16[16,64,640]{2,1,0:T(8,128)(2,1)S(1)} all-to-all(bf16[16,64,640]{2,1,0:T(8,128)(2,1)S(1)} %shard_map.49), channel_id=1, replica_groups=mesh['xl'=2,'y'=4,'c'=2,'xh'=2,'z'=16] {'xl','y','xh'}, dimensions={0} | all-to-all | bytes 2621440 | tf_op jit(solution)/shard_map/all_to_all | solution.py:230
  87.6 0.0 copy-start.1
  87.6 0.0 copy-start.2
  87.6 0.2 shard_map.50
  87.8 4.0 %all_gather.23.qkv_ref = bf16[1024,384]{1,0:T(8,128)(2,1)S(1)} all-gather(bf16[512,384]{1,0:T(8,128)(2,1)S(1)} %bitcast.11), channel_id=1, replica_groups=mesh['xl'=2,'y'=4,'c'=2,'xh'=2,'z'=16] {'c'}, dimensions={0}, use_global_device_ids=true | all-gather | bytes 1179648 | tf_op jit(solution)/shard_map/all_gather | solution.py:232
  91.8 0.0 copy-done.1
  91.8 0.0 copy-done.2
  91.8 1.4 %shard_map.51 = bf16[4,64,128]{2,1,0:T(8,128)(2,1)S(1)} custom-call(s32[3,16]{1,0:T(4,128)S(1)} %copy-done.1, s32[3,4]{1,0:T(4,128)S(1)} %copy-done.2, bf16[1024,384]{1,0:T(8,128)(2,1)S(1)} %all_gather.23.qkv_ref), custom_call_target="tpu_custom_call" | custom-call | flops 200000000 | bytes 1000000 | tf_op jit(solution)/shard_map/pallas_call | solution.py:234
  93.3 6.8 %all_to_all.16 = bf16[4,64,128]{2,1,0:T(8,128)(2,1)S(1)} all-to-all(bf16[4,64,128]{2,1,0:T(8,128)(2,1)S(1)} %shard_map.51), channel_id=1, replica_groups=mesh['xl'=2,'y'=4,'c'=2,'xh'=2,'z'=16] {'y'}, dimensions={0} | all-to-all | bytes 131072 | tf_op jit(solution)/shard_map/all_to_all | solution.py:242
  100.1 0.6 slice_bitcast_fusion
Async XLA Ops:
  12.7 0.9 copy-start
  15.0 38.1 %all-to-all-start = ((bf16[8,320,384]{2,1,0:T(8,128)(2,1)}), bf16[8,320,384]{2,1,0:T(8,128)(2,1)S(1)}, u32[]{:S(2)}, u32[]{:S(2)}) async-start(bf16[8,320,384]{2,1,0:T(8,128)(2,1)} %shard_map.46), calls=%async_computation | async-start | bytes 3932160 | tf_op jit(solution)/shard_map/all_to_all | solution.py:206
  87.6 4.2 %copy-start.1 = (s32[3,16]{1,0:T(4,128)S(1)}, s32[3,16]{1,0:T(4,128)}, u32[]{:S(2)}) copy-start(s32[3,16]{1,0:T(4,128)} %destination_ref.1) | copy-start | bytes 580
  87.6 4.2 %copy-start.2 = (s32[3,4]{1,0:T(4,128)S(1)}, s32[3,4]{1,0:T(4,128)}, u32[]{:S(2)}) copy-start(s32[3,4]{1,0:T(4,128)} %lengths_ref.1) | copy-start | bytes 148

commit v2 on v1

--- a/solution.py
+++ b/solution.py
@@ -94,25 +94,26 @@
             total = keep_ref[rows, head * QKV : (head + 1) * QKV]
             total = jnp.concatenate([total[:, : 2 * HD] + scored, total[:, 2 * HD :] + value], axis=1)
             rounded, rest = split(total)
+            for xl in range(2):
+                block, at = slice(xl * HALF, (xl + 1) * HALF), slice(p * HALF, (p + 1) * HALF)
+                out_ref[xl * 2 + head, at, :QKV] = rounded[block]
+                out_ref[xl * 2 + head, at, QKV:] = rest[block]
+
+
+def total_kernel(parts_ref, out_ref):
+    for p in range(NPACK):
+        at = slice(p * HALF, (p + 1) * HALF)
+        for xh in range(2):
+            scored, value = joined(parts_ref[xh, at])
+            more_scored, more_value = joined(parts_ref[2 + xh, at])
+            scored = (scored + more_scored).astype(jnp.bfloat16)
+            value = (value + more_value).astype(jnp.bfloat16)
+            half = slice(xh * HALF, (xh + 1) * HALF)
             for y, pack in enumerate(PACK_OF):
                 if pack == p:
                     for xl in range(2):
-                        out_ref[xl * 8 + y * 2 + head, :, :QKV] = rounded
-                        out_ref[xl * 8 + y * 2 + head, :, QKV:] = rest
-
-
-def total_kernel(parts_ref, out_ref):
-    for y in range(4):
-        for xh in range(2):
-            at = y * 2 + xh
-            scored, value = joined(parts_ref[at])
-            more_scored, more_value = joined(parts_ref[8 + at])
-            scored = (scored + more_scored).astype(jnp.bfloat16)
-            value = (value + more_value).astype(jnp.bfloat16)
-            for xl in range(2):
-                block, half = slice(xl * HALF, (xl + 1) * HALF), slice(xh * HALF, (xh + 1) * HALF)
-                out_ref[xl * 4 + y, half, : 2 * HD] = scored[block]
-                out_ref[xl * 4 + y, half, 2 * HD :] = value[block]
+                        out_ref[xl * 4 + y, half, : 2 * HD] = scored
+                        out_ref[xl * 4 + y, half, 2 * HD :] = value
 
 
 def row_of(at):
@@ -224,11 +225,12 @@
     got = lax.all_gather(give, "c", axis=0)
     spread = call(
         pair_kernel,
-        jax.ShapeDtypeStruct((16, BLK, SENT), half_type),
+        jax.ShapeDtypeStruct((4, NPACK * HALF, SENT), half_type),
         [whole(), whole()],
     )(keep, got)
-    parts = lax.all_to_all(spread, ("xl", "y", "xh"), 0, 0, tiled=True)
-    blocks = call(total_kernel, jax.ShapeDtypeStruct((8, BLK, QKV), half_type), [whole()])(parts)
+    parts = lax.all_to_all(spread, ("xl", "xh"), 0, 0, tiled=True)
+    spread = call(total_kernel, jax.ShapeDtypeStruct((8, BLK, QKV), half_type), [whole()])(parts)
+    blocks = lax.all_to_all(spread, ("xl", "y"), 0, 0, tiled=True)
     blocks = lax.all_gather(blocks.reshape(8 * BLK, QKV), "c", axis=0, tiled=True)
 
     attended = call(

time: 101 us -> 99.4 us (0.984)
  blocking collectives: 90.8 us -> 89.3 us
    all_to_all x1 -> x2, blocking collectives: 25.6 us -> 23.1 us  [the longest x1 12.4 us: shards(): parts = lax.all_to_all(spread, ('xl', 'xh'), 0, 0, tiled=True)]
where the time goes in v2:
time: 99.4 us; the launch traced here: 99.1 us
  blocking collectives  89.3 us (90%)
  Pallas kernels  4.57 us (5%)
  starting transfers between devices  3.61 us (4%)
  local copies, waits for them, and re-layouts  1.58 us (2%)
    all_gather x1, blocking collectives, shards(): rows = lax.all_gather(rows, 'z', axis=0, tiled=True)  34.3 us
    all_gather x1, blocking collectives, shards(): near = lax.all_gather(patches, ('xl', 'c'), axis=0)  12.7 us
    all_to_all x1, blocking collectives, shards(): parts = lax.all_to_all(spread, ('xl', 'xh'), 0, 0, tiled=True)  12.4 us
    all_to_all x1, blocking collectives, shards(): blocks = lax.all_to_all(spread, ('xl', 'y'), 0, 0, tiled=True)  10.7 us
    all_gather x1, blocking collectives, shards(): got = lax.all_gather(give, 'c', axis=0)  7.41 us
    all_to_all x1, blocking collectives, shards(): home = lax.all_to_all(attended, 'y', 0, 0, tiled=True)  6.84 us
    all_gather x1, blocking collectives, shards(): lax.all_gather(blocks.reshape(8 * BLK, QKV), 'c', axis=0, tiled=True)  4.97 us
    all_to_all x1, starting transfers between devices, shards(): weight_set = lax.all_to_all(slots, ('y', 'xh'), 0, 0, tiled=True)  3.61 us
  transfers between devices with their start and end apart: 1, of which 0 were waited for; matrix products, arithmetic and copies ran while one was open for 0% of the time, Pallas kernels for 0%

profile of v2, /device:TPU:1, one launch (start us, length us, event | category | flops | bytes accessed | tf_op | source)
XLA Modules:
  0.0 99.1 jit_solution(607899958961911704)
XLA Ops:
  0.0 12.7 %all-gather = bf16[12,2,5120]{2,1,0:T(2,128)(2,1)S(1)} all-gather(bf16[3,2,5120]{2,1,0:T(2,128)(2,1)} %param.4), channel_id=2, replica_groups=mesh['xl'=2,'y'=4,'c'=2,'xh'=2,'z'=16] {'xl','c'}, dimensions={0}, use_global_device_ids=true | all-gather | bytes 307200 | tf_op jit(solution)/shard_map/all_gather | solution.py:205
  12.7 0.0 copy-start
  12.7 0.9 copy-done
  13.6 1.4 %shard_map.46 = bf16[8,320,384]{2,1,0:T(8,128)(2,1)} custom-call(bf16[320,384]{1,0:T(8,128)(2,1)S(1)} %bitcast.12), custom_call_target="tpu_custom_call" | custom-call | bytes 1000000 | tf_op jit(solution)/shard_map/pallas_call | solution.py:198
  15.0 3.6 %all-to-all-start = ((bf16[8,320,384]{2,1,0:T(8,128)(2,1)}), bf16[8,320,384]{2,1,0:T(8,128)(2,1)S(1)}, u32[]{:S(2)}, u32[]{:S(2)}) async-start(bf16[8,320,384]{2,1,0:T(8,128)(2,1)} %shard_map.46), calls=%async_computation | async-start | bytes 3932160 | tf_op jit(solution)/shard_map/all_to_all | solution.py:207
  18.6 0.2 shard_map.47
  18.8 34.3 %all_gather.20.x_ref = bf16[384,1280]{1,0:T(8,128)(2,1)S(1)} all-gather(bf16[24,1280]{1,0:T(8,128)(2,1)S(1)} %shard_map.47), channel_id=1, replica_groups=mesh['xl'=2,'y'=4,'c'=2,'xh'=2,'z'=16] {'z'}, dimensions={0}, use_global_device_ids=true | all-gather | bytes 1044480 | tf_op jit(solution)/shard_map/all_gather | solution.py:212
  53.1 0.0 all-to-all-done
  53.1 1.3 %shard_map.48 = (f32[192,768]{1,0:T(8,128)S(1)}, bf16[192,1280]{1,0:T(8,128)(2,1)S(1)}) custom-call(bf16[384,1280]{1,0:T(8,128)(2,1)S(1)} %all_gather.20.x_ref, bf16[4,2,320,384]{3,2,1,0:T(8,128)(2,1)S(1)} %bitcast.10), custom_call_target="tpu_custom_call" | custom-call | flops 1000000000 | bytes 4000000 | tf_op jit(solution)/shard_map/pallas_call | solution.py:214
  54.4 7.4 %all-gather.1 = bf16[384,1280]{1,0:T(8,128)(2,1)S(1)} all-gather(bf16[192,1280]{1,0:T(8,128)(2,1)S(1)} %get-tuple-element.12), channel_id=3, replica_groups=mesh['xl'=2,'y'=4,'c'=2,'xh'=2,'z'=16] {'c'}, dimensions={0}, use_global_device_ids=true | all-gather | bytes 1474560 | tf_op jit(solution)/shard_map/all_gather | solution.py:225
  61.8 0.1 shard_map.49
  62.0 0.0 copy-start.1
  62.0 0.0 copy-start.2
  62.0 12.4 %all_to_all.20.parts_ref = bf16[4,96,640]{2,1,0:T(8,128)(2,1)S(1)} all-to-all(bf16[4,96,640]{2,1,0:T(8,128)(2,1)S(1)} %shard_map.49), channel_id=1, replica_groups=mesh['xl'=2,'y'=4,'c'=2,'xh'=2,'z'=16] {'xl','xh'}, dimensions={0} | all-to-all | bytes 983040 | tf_op jit(solution)/shard_map/all_to_all | solution.py:231
  74.4 0.1 shard_map.50
  74.5 10.7 %all_to_all.21 = bf16[8,64,384]{2,1,0:T(8,128)(2,1)S(1)} all-to-all(bf16[8,64,384]{2,1,0:T(8,128)(2,1)S(1)} %shard_map.50), channel_id=1, replica_groups=mesh['xl'=2,'y'=4,'c'=2,'xh'=2,'z'=16] {'xl','y'}, dimensions={0} | all-to-all | bytes 786432 | tf_op jit(solution)/shard_map/all_to_all | solution.py:233
  85.2 5.0 %all_gather.23.qkv_ref = bf16[1024,384]{1,0:T(8,128)(2,1)S(1)} all-gather(bf16[512,384]{1,0:T(8,128)(2,1)S(1)} %bitcast.13), channel_id=1, replica_groups=mesh['xl'=2,'y'=4,'c'=2,'xh'=2,'z'=16] {'c'}, dimensions={0}, use_global_device_ids=true | all-gather | bytes 1179648 | tf_op jit(solution)/shard_map/all_gather | solution.py:234
  90.2 0.0 copy-done.1
  90.2 0.0 copy-done.2
  90.2 1.4 %shard_map.51 = bf16[4,64,128]{2,1,0:T(8,128)(2,1)S(1)} custom-call(s32[3,16]{1,0:T(4,128)S(1)} %copy-done.1, s32[3,4]{1,0:T(4,128)S(1)} %copy-done.2, bf16[1024,384]{1,0:T(8,128)(2,1)S(1)} %all_gather.23.qkv_ref), custom_call_target="tpu_custom_call" | custom-call | flops 200000000 | bytes 1000000 | tf_op jit(solution)/shard_map/pallas_call | solution.py:236
  91.6 6.8 %all_to_all.22 = bf16[4,64,128]{2,1,0:T(8,128)(2,1)S(1)} all-to-all(bf16[4,64,128]{2,1,0:T(8,128)(2,1)S(1)} %shard_map.51), channel_id=1, replica_groups=mesh['xl'=2,'y'=4,'c'=2,'xh'=2,'z'=16] {'y'}, dimensions={0} | all-to-all | bytes 131072 | tf_op jit(solution)/shard_map/all_to_all | solution.py:244
  98.5 0.6 slice_bitcast_fusion
Async XLA Ops:
  12.7 0.9 copy-start
  15.0 38.1 %all-to-all-start = ((bf16[8,320,384]{2,1,0:T(8,128)(2,1)}), bf16[8,320,384]{2,1,0:T(8,128)(2,1)S(1)}, u32[]{:S(2)}, u32[]{:S(2)}) async-start(bf16[8,320,384]{2,1,0:T(8,128)(2,1)} %shard_map.46), calls=%async_computation | async-start | bytes 3932160 | tf_op jit(solution)/shard_map/all_to_all | solution.py:207
  62.0 28.2 %copy-start.1 = (s32[3,16]{1,0:T(4,128)S(1)}, s32[3,16]{1,0:T(4,128)}, u32[]{:S(2)}) copy-start(s32[3,16]{1,0:T(4,128)} %destination_ref.1) | copy-start | bytes 580
  62.0 28.2 %copy-start.2 = (s32[3,4]{1,0:T(4,128)S(1)}, s32[3,4]{1,0:T(4,128)}, u32[]{:S(2)}) copy-start(s32[3,4]{1,0:T(4,128)} %lengths_ref.1) | copy-start | bytes 148

commit v3 on v2

--- a/solution.py
+++ b/solution.py
@@ -66,7 +66,7 @@
             x_ref[...], w_ref[:, head].reshape(KSET, QKV), preferred_element_type=jnp.float32
         )
         for k in range(3):
-            product_ref[k] = product[:, k * HD : (k + 1) * HD]
+            product_ref[k, : 4 * LOCAL * NZ] = product[:, k * HD : (k + 1) * HD]
             columns = slice(head * QKV + k * HD, head * QKV + (k + 1) * HD)
             sent = slice(head * SENT + k * HD, head * SENT + (k + 1) * HD)
             remainder = slice(head * SENT + QKV + k * HD, head * SENT + QKV + (k + 1) * HD)
@@ -218,7 +218,7 @@
             jax.ShapeDtypeStruct((ROWS, 2 * SENT), half_type),
         ),
         [whole(), whole()],
-        [pltpu.VMEM((3, 4 * LOCAL * NZ, HD), jnp.float32)],
+        [pltpu.VMEM((3, 4 * LOCAL * (NZ + 1), HD), jnp.float32)],
         cost=(10**9, 4 * 10**6, 0),
     )(rows, weight_set.reshape(4, 2, PIECE, QKV))
 
@@ -237,7 +237,7 @@
         attend_kernel,
         jax.ShapeDtypeStruct((4, BLK, HD), half_type),
         [whole(pltpu.SMEM)] * 2 + [whole()],
-        [pltpu.VMEM((4 * BLK, HD), jnp.float32)],
+        [pltpu.VMEM((4 * BLK + 8, HD), jnp.float32)],
         cost=(2 * 10**8, 10**6, 3 * 10**5),
     )(destination, image_lengths, blocks)
 

time: 99.4 us -> 99.5 us (level)
  no operation moved by 1% of the time
where the time goes in v3:
time: 99.5 us; the launch traced here: 99.1 us
  blocking collectives  89.3 us (90%)
  Pallas kernels  4.6 us (5%)
  starting transfers between devices  3.61 us (4%)
  local copies, waits for them, and re-layouts  1.58 us (2%)
    all_gather x1, blocking collectives, shards(): rows = lax.all_gather(rows, 'z', axis=0, tiled=True)  34.3 us
    all_gather x1, blocking collectives, shards(): near = lax.all_gather(patches, ('xl', 'c'), axis=0)  12.7 us
    all_to_all x1, blocking collectives, shards(): parts = lax.all_to_all(spread, ('xl', 'xh'), 0, 0, tiled=True)  12.4 us
    all_to_all x1, blocking collectives, shards(): blocks = lax.all_to_all(spread, ('xl', 'y'), 0, 0, tiled=True)  10.7 us
    all_gather x1, blocking collectives, shards(): got = lax.all_gather(give, 'c', axis=0)  7.4 us
    all_to_all x1, blocking collectives, shards(): home = lax.all_to_all(attended, 'y', 0, 0, tiled=True)  6.84 us
    all_gather x1, blocking collectives, shards(): lax.all_gather(blocks.reshape(8 * BLK, QKV), 'c', axis=0, tiled=True)  4.97 us
    all_to_all x1, starting transfers between devices, shards(): weight_set = lax.all_to_all(slots, ('y', 'xh'), 0, 0, tiled=True)  3.61 us
  transfers between devices with their start and end apart: 1, of which 0 were waited for; matrix products, arithmetic and copies ran while one was open for 0% of the time, Pallas kernels for 0%

profile of v3, /device:TPU:1, one launch (start us, length us, event | category | flops | bytes accessed | tf_op | source)
XLA Modules:
  0.0 99.1 jit_solution(14782568465679875281)
XLA Ops:
  0.0 12.7 %all-gather = bf16[12,2,5120]{2,1,0:T(2,128)(2,1)S(1)} all-gather(bf16[3,2,5120]{2,1,0:T(2,128)(2,1)} %param.4), channel_id=2, replica_groups=mesh['xl'=2,'y'=4,'c'=2,'xh'=2,'z'=16] {'xl','c'}, dimensions={0}, use_global_device_ids=true | all-gather | bytes 307200 | tf_op jit(solution)/shard_map/all_gather | solution.py:205
  12.7 0.0 copy-start
  12.7 0.9 copy-done
  13.6 1.4 %shard_map.46 = bf16[8,320,384]{2,1,0:T(8,128)(2,1)} custom-call(bf16[320,384]{1,0:T(8,128)(2,1)S(1)} %bitcast.12), custom_call_target="tpu_custom_call" | custom-call | bytes 1000000 | tf_op jit(solution)/shard_map/pallas_call | solution.py:198
  15.0 3.6 %all-to-all-start = ((bf16[8,320,384]{2,1,0:T(8,128)(2,1)}), bf16[8,320,384]{2,1,0:T(8,128)(2,1)S(1)}, u32[]{:S(2)}, u32[]{:S(2)}) async-start(bf16[8,320,384]{2,1,0:T(8,128)(2,1)} %shard_map.46), calls=%async_computation | async-start | bytes 3932160 | tf_op jit(solution)/shard_map/all_to_all | solution.py:207
  18.6 0.2 shard_map.47
  18.8 34.3 %all_gather.20.x_ref = bf16[384,1280]{1,0:T(8,128)(2,1)S(1)} all-gather(bf16[24,1280]{1,0:T(8,128)(2,1)S(1)} %shard_map.47), channel_id=1, replica_groups=mesh['xl'=2,'y'=4,'c'=2,'xh'=2,'z'=16] {'z'}, dimensions={0}, use_global_device_ids=true | all-gather | bytes 1044480 | tf_op jit(solution)/shard_map/all_gather | solution.py:212
  53.1 0.0 all-to-all-done
  53.1 1.4 %shard_map.48 = (f32[192,768]{1,0:T(8,128)S(1)}, bf16[192,1280]{1,0:T(8,128)(2,1)S(1)}) custom-call(bf16[384,1280]{1,0:T(8,128)(2,1)S(1)} %all_gather.20.x_ref, bf16[4,2,320,384]{3,2,1,0:T(8,128)(2,1)S(1)} %bitcast.10), custom_call_target="tpu_custom_call" | custom-call | flops 1000000000 | bytes 4000000 | tf_op jit(solution)/shard_map/pallas_call | solution.py:214
  54.4 7.4 %all-gather.1 = bf16[384,1280]{1,0:T(8,128)(2,1)S(1)} all-gather(bf16[192,1280]{1,0:T(8,128)(2,1)S(1)} %get-tuple-element.12), channel_id=3, replica_groups=mesh['xl'=2,'y'=4,'c'=2,'xh'=2,'z'=16] {'c'}, dimensions={0}, use_global_device_ids=true | all-gather | bytes 1474560 | tf_op jit(solution)/shard_map/all_gather | solution.py:225
  61.8 0.1 shard_map.49
  62.0 0.0 copy-start.1
  62.0 0.0 copy-start.2
  62.0 12.4 %all_to_all.20.parts_ref = bf16[4,96,640]{2,1,0:T(8,128)(2,1)S(1)} all-to-all(bf16[4,96,640]{2,1,0:T(8,128)(2,1)S(1)} %shard_map.49), channel_id=1, replica_groups=mesh['xl'=2,'y'=4,'c'=2,'xh'=2,'z'=16] {'xl','xh'}, dimensions={0} | all-to-all | bytes 983040 | tf_op jit(solution)/shard_map/all_to_all | solution.py:231
  74.4 0.1 shard_map.50
  74.5 10.7 %all_to_all.21 = bf16[8,64,384]{2,1,0:T(8,128)(2,1)S(1)} all-to-all(bf16[8,64,384]{2,1,0:T(8,128)(2,1)S(1)} %shard_map.50), channel_id=1, replica_groups=mesh['xl'=2,'y'=4,'c'=2,'xh'=2,'z'=16] {'xl','y'}, dimensions={0} | all-to-all | bytes 786432 | tf_op jit(solution)/shard_map/all_to_all | solution.py:233
  85.2 5.0 %all_gather.23.qkv_ref = bf16[1024,384]{1,0:T(8,128)(2,1)S(1)} all-gather(bf16[512,384]{1,0:T(8,128)(2,1)S(1)} %bitcast.13), channel_id=1, replica_groups=mesh['xl'=2,'y'=4,'c'=2,'xh'=2,'z'=16] {'c'}, dimensions={0}, use_global_device_ids=true | all-gather | bytes 1179648 | tf_op jit(solution)/shard_map/all_gather | solution.py:234
  90.2 0.0 copy-done.1
  90.2 0.0 copy-done.2
  90.2 1.4 %shard_map.51 = bf16[4,64,128]{2,1,0:T(8,128)(2,1)S(1)} custom-call(s32[3,16]{1,0:T(4,128)S(1)} %copy-done.1, s32[3,4]{1,0:T(4,128)S(1)} %copy-done.2, bf16[1024,384]{1,0:T(8,128)(2,1)S(1)} %all_gather.23.qkv_ref), custom_call_target="tpu_custom_call" | custom-call | flops 200000000 | bytes 1000000 | tf_op jit(solution)/shard_map/pallas_call | solution.py:236
  91.7 6.8 %all_to_all.22 = bf16[4,64,128]{2,1,0:T(8,128)(2,1)S(1)} all-to-all(bf16[4,64,128]{2,1,0:T(8,128)(2,1)S(1)} %shard_map.51), channel_id=1, replica_groups=mesh['xl'=2,'y'=4,'c'=2,'xh'=2,'z'=16] {'y'}, dimensions={0} | all-to-all | bytes 131072 | tf_op jit(solution)/shard_map/all_to_all | solution.py:244
  98.5 0.6 slice_bitcast_fusion
Async XLA Ops:
  12.7 0.9 copy-start
  15.0 38.1 %all-to-all-start = ((bf16[8,320,384]{2,1,0:T(8,128)(2,1)}), bf16[8,320,384]{2,1,0:T(8,128)(2,1)S(1)}, u32[]{:S(2)}, u32[]{:S(2)}) async-start(bf16[8,320,384]{2,1,0:T(8,128)(2,1)} %shard_map.46), calls=%async_computation | async-start | bytes 3932160 | tf_op jit(solution)/shard_map/all_to_all | solution.py:207
  62.0 28.2 %copy-start.1 = (s32[3,16]{1,0:T(4,128)S(1)}, s32[3,16]{1,0:T(4,128)}, u32[]{:S(2)}) copy-start(s32[3,16]{1,0:T(4,128)} %destination_ref.1) | copy-start | bytes 580
  62.0 28.2 %copy-start.2 = (s32[3,4]{1,0:T(4,128)S(1)}, s32[3,4]{1,0:T(4,128)}, u32[]{:S(2)}) copy-start(s32[3,4]{1,0:T(4,128)} %lengths_ref.1) | copy-start | bytes 148

commit v4 on v3

--- a/solution.py
+++ b/solution.py
@@ -13,7 +13,6 @@
 IMGS = 4
 NBLK = 16
 QKV = 3 * HD
-SENT = 5 * HD
 NZ = 16
 PIECE = D // 16
 KSET = 4 * PIECE
@@ -47,18 +46,6 @@
     out_ref[...] = jnp.concatenate(cut, axis=1).astype(jnp.bfloat16)
 
 
-def split(product):
-    whole_part = product.astype(jnp.bfloat16)
-    scored = slice(0, 2 * HD)
-    rest = (product[:, scored] - whole_part[:, scored].astype(jnp.float32)).astype(jnp.bfloat16)
-    return whole_part, rest
-
-
-def joined(sent):
-    scored = sent[:, : 2 * HD].astype(jnp.float32) + sent[:, QKV:].astype(jnp.float32)
-    return scored, sent[:, 2 * HD : QKV].astype(jnp.float32)
-
-
 def project_kernel(x_ref, w_ref, keep_ref, give_ref, product_ref):
     own = lax.axis_index("c")
     for head in range(2):
@@ -68,8 +55,6 @@
         for k in range(3):
             product_ref[k, : 4 * LOCAL * NZ] = product[:, k * HD : (k + 1) * HD]
             columns = slice(head * QKV + k * HD, head * QKV + (k + 1) * HD)
-            sent = slice(head * SENT + k * HD, head * SENT + (k + 1) * HD)
-            remainder = slice(head * SENT + QKV + k * HD, head * SENT + QKV + (k + 1) * HD)
             for p in range(NPACK):
                 for xl in range(2):
                     for i in range(2):
@@ -78,42 +63,28 @@
                         mine = product_ref[k, pl.ds(first + own * LOCAL, NZ, stride=4 * LOCAL), :]
                         theirs = product_ref[k, pl.ds(first + (1 - own) * LOCAL, NZ, stride=4 * LOCAL), :]
                         keep_ref[at : at + NZ, columns] = mine
-                        rounded = theirs.astype(jnp.bfloat16)
-                        give_ref[at : at + NZ, sent] = rounded
-                        if k < 2:
-                            rest = theirs - rounded.astype(jnp.float32)
-                            give_ref[at : at + NZ, remainder] = rest.astype(jnp.bfloat16)
+                        give_ref[at : at + NZ, columns] = theirs
 
 
 def pair_kernel(keep_ref, got_ref, out_ref):
-    other = 1 - lax.axis_index("c")
     for p in range(NPACK):
-        rows = slice(p * BLK, (p + 1) * BLK)
-        for head in range(2):
-            scored, value = joined(got_ref[other, rows, head * SENT : (head + 1) * SENT])
-            total = keep_ref[rows, head * QKV : (head + 1) * QKV]
-            total = jnp.concatenate([total[:, : 2 * HD] + scored, total[:, 2 * HD :] + value], axis=1)
-            rounded, rest = split(total)
-            for xl in range(2):
-                block, at = slice(xl * HALF, (xl + 1) * HALF), slice(p * HALF, (p + 1) * HALF)
-                out_ref[xl * 2 + head, at, :QKV] = rounded[block]
-                out_ref[xl * 2 + head, at, QKV:] = rest[block]
+        for xl in range(2):
+            start = p * BLK + xl * HALF
+            for head in range(2):
+                columns = slice(head * QKV, (head + 1) * QKV)
+                total = keep_ref[start : start + HALF, columns] + got_ref[start : start + HALF, columns]
+                out_ref[xl * 2 + head, p * HALF : (p + 1) * HALF] = total
 
 
 def total_kernel(parts_ref, out_ref):
     for p in range(NPACK):
         at = slice(p * HALF, (p + 1) * HALF)
         for xh in range(2):
-            scored, value = joined(parts_ref[xh, at])
-            more_scored, more_value = joined(parts_ref[2 + xh, at])
-            scored = (scored + more_scored).astype(jnp.bfloat16)
-            value = (value + more_value).astype(jnp.bfloat16)
-            half = slice(xh * HALF, (xh + 1) * HALF)
+            total = (parts_ref[xh, at] + parts_ref[2 + xh, at]).astype(jnp.bfloat16)
             for y, pack in enumerate(PACK_OF):
                 if pack == p:
                     for xl in range(2):
-                        out_ref[xl * 4 + y, half, : 2 * HD] = scored
-                        out_ref[xl * 4 + y, half, 2 * HD :] = value
+                        out_ref[xl * 4 + y, xh * HALF : (xh + 1) * HALF] = total
 
 
 def row_of(at):
@@ -215,17 +186,17 @@
         project_kernel,
         (
             jax.ShapeDtypeStruct((ROWS, 2 * QKV), jnp.float32),
-            jax.ShapeDtypeStruct((ROWS, 2 * SENT), half_type),
+            jax.ShapeDtypeStruct((ROWS, 2 * QKV), jnp.float32),
         ),
         [whole(), whole()],
         [pltpu.VMEM((3, 4 * LOCAL * (NZ + 1), HD), jnp.float32)],
         cost=(10**9, 4 * 10**6, 0),
     )(rows, weight_set.reshape(4, 2, PIECE, QKV))
 
-    got = lax.all_gather(give, "c", axis=0)
+    got = lax.ppermute(give, "c", [(0, 1), (1, 0)])
     spread = call(
         pair_kernel,
-        jax.ShapeDtypeStruct((4, NPACK * HALF, SENT), half_type),
+        jax.ShapeDtypeStruct((4, NPACK * HALF, QKV), jnp.float32),
         [whole(), whole()],
     )(keep, got)
     parts = lax.all_to_all(spread, ("xl", "xh"), 0, 0, tiled=True)

time: 99.5 us -> 102 us (1.025)
  starting transfers between devices: 3.61 us -> 10.8 us
  blocking collectives: 89.3 us -> 83 us
  waiting for transfers between devices: 0.01 us -> 1.61 us
    all_gather x1 -> x0, blocking collectives: 7.4 us -> none  [shards(): got = lax.all_gather(give, 'c', axis=0)]
    ppermute x0 -> x1, starting transfers between devices: none -> 7.17 us  [shards(): got = lax.ppermute(give, 'c', [(0, 1), (1, 0)])]
    ppermute x0 -> x1, waiting for transfers between devices: none -> 1.61 us  [shards(): got = lax.ppermute(give, 'c', [(0, 1), (1, 0)])]
    all_to_all x1, blocking collectives: 12.4 us -> 13.5 us  [shards(): parts = lax.all_to_all(spread, ('xl', 'xh'), 0, 0, tiled=True)]
  transfers between devices with their start and end apart: 1 -> 2, of which waited for: 0 -> 1; matrix products, arithmetic and copies ran while one was open for 0% -> 0% of each run, Pallas kernels for 0% -> 0%
where the time goes in v4:
time: 102 us
  blocking collectives  83 us (81%)
  starting transfers between devices  10.8 us (11%)
  Pallas kernels  4.45 us (4%)
  waiting for transfers between devices  1.61 us (2%)
  local copies, waits for them, and re-layouts  1.58 us (2%)
    all_gather x1, blocking collectives, shards(): rows = lax.all_gather(rows, 'z', axis=0, tiled=True)  34.3 us
    all_to_all x1, blocking collectives, shards(): parts = lax.all_to_all(spread, ('xl', 'xh'), 0, 0, tiled=True)  13.5 us
    all_gather x1, blocking collectives, shards(): near = lax.all_gather(patches, ('xl', 'c'), axis=0)  12.7 us
    all_to_all x1, blocking collectives, shards(): blocks = lax.all_to_all(spread, ('xl', 'y'), 0, 0, tiled=True)  10.7 us
    ppermute x1, starting transfers between devices, shards(): got = lax.ppermute(give, 'c', [(0, 1), (1, 0)])  7.17 us
    all_to_all x1, blocking collectives, shards(): home = lax.all_to_all(attended, 'y', 0, 0, tiled=True)  6.84 us
    all_gather x1, blocking collectives, shards(): lax.all_gather(blocks.reshape(8 * BLK, QKV), 'c', axis=0, tiled=True)  5 us
    all_to_all x1, starting transfers between devices, shards(): weight_set = lax.all_to_all(slots, ('y', 'xh'), 0, 0, tiled=True)  3.61 us
  transfers between devices with their start and end apart: 2, of which 1 were waited for; matrix products, arithmetic and copies ran while one was open for 0% of the time, Pallas kernels for 0%

profile of v4, /device:TPU:1, one launch (start us, length us, event | category | flops | bytes accessed | tf_op | source)
XLA Modules:
  0.0 101.5 jit_solution(2013726178649058446)
XLA Ops:
  0.0 12.7 %all-gather = bf16[12,2,5120]{2,1,0:T(2,128)(2,1)S(1)} all-gather(bf16[3,2,5120]{2,1,0:T(2,128)(2,1)} %param.4), channel_id=2, replica_groups=mesh['xl'=2,'y'=4,'c'=2,'xh'=2,'z'=16] {'xl','c'}, dimensions={0}, use_global_device_ids=true | all-gather | bytes 307200 | tf_op jit(solution)/shard_map/all_gather | solution.py:176
  12.7 0.0 copy-start
  12.7 0.9 copy-done
  13.6 1.4 %shard_map.46 = bf16[8,320,384]{2,1,0:T(8,128)(2,1)} custom-call(bf16[320,384]{1,0:T(8,128)(2,1)S(1)} %bitcast.10), custom_call_target="tpu_custom_call" | custom-call | bytes 1000000 | tf_op jit(solution)/shard_map/pallas_call | solution.py:169
  15.0 3.6 %all-to-all-start = ((bf16[8,320,384]{2,1,0:T(8,128)(2,1)}), bf16[8,320,384]{2,1,0:T(8,128)(2,1)S(1)}, u32[]{:S(2)}, u32[]{:S(2)}) async-start(bf16[8,320,384]{2,1,0:T(8,128)(2,1)} %shard_map.46), calls=%async_computation | async-start | bytes 3932160 | tf_op jit(solution)/shard_map/all_to_all | solution.py:178
  18.6 0.2 shard_map.47
  18.8 34.3 %all_gather.14.x_ref = bf16[384,1280]{1,0:T(8,128)(2,1)S(1)} all-gather(bf16[24,1280]{1,0:T(8,128)(2,1)S(1)} %shard_map.47), channel_id=1, replica_groups=mesh['xl'=2,'y'=4,'c'=2,'xh'=2,'z'=16] {'z'}, dimensions={0}, use_global_device_ids=true | all-gather | bytes 1044480 | tf_op jit(solution)/shard_map/all_gather | solution.py:183
  53.1 0.0 all-to-all-done
  53.1 1.3 %shard_map.48 = (f32[192,768]{1,0:T(8,128)S(1)}, f32[192,768]{1,0:T(8,128)S(1)}) custom-call(bf16[384,1280]{1,0:T(8,128)(2,1)S(1)} %all_gather.14.x_ref, bf16[4,2,320,384]{3,2,1,0:T(8,128)(2,1)S(1)} %bitcast.8), custom_call_target="tpu_custom_call" | custom-call | flops 1000000000 | bytes 4000000 | tf_op jit(solution)/shard_map/pallas_call | solution.py:185
  54.4 7.2 %collective-permute-start = (f32[192,768]{1,0:T(8,128)S(1)}, f32[192,768]{1,0:T(8,128)S(1)}, u32[]{:S(2)}, u32[]{:S(2)}) collective-permute-start(f32[192,768]{1,0:T(8,128)S(1)} %get-tuple-element.12), channel_id=1, source_target_pairs={{0,32},{32,0},{1,33},{33,1},{2,34},{34,2},{3,35},{35,3},{4,36},{36... | collective-permute-start | bytes 1769480 | tf_op jit(solution)/shard_map/ppermute | solution.py:196
  61.6 1.6 %collective-permute-done.got_ref = f32[192,768]{1,0:T(8,128)S(1)} collective-permute-done((f32[192,768]{1,0:T(8,128)S(1)}, f32[192,768]{1,0:T(8,128)S(1)}, u32[]{:S(2)}, u32[]{:S(2)}) %collective-permute-start) | collective-permute-done | bytes 589856 | tf_op jit(solution)/shard_map/ppermute | solution.py:196
  63.2 0.1 shard_map.49
  63.3 0.0 copy-start.1
  63.3 0.0 copy-start.2
  63.3 13.5 %all_to_all.20.parts_ref = f32[4,96,384]{2,1,0:T(8,128)S(1)} all-to-all(f32[4,96,384]{2,1,0:T(8,128)S(1)} %shard_map.49), channel_id=1, replica_groups=mesh['xl'=2,'y'=4,'c'=2,'xh'=2,'z'=16] {'xl','xh'}, dimensions={0} | all-to-all | bytes 1179648 | tf_op jit(solution)/shard_map/all_to_all | solution.py:202
  76.9 10.7 %all_to_all.21 = bf16[8,64,384]{2,1,0:T(8,128)(2,1)S(1)} all-to-all(bf16[8,64,384]{2,1,0:T(8,128)(2,1)S(1)} %shard_map.50), channel_id=1, replica_groups=mesh['xl'=2,'y'=4,'c'=2,'xh'=2,'z'=16] {'xl','y'}, dimensions={0} | all-to-all | bytes 786432 | tf_op jit(solution)/shard_map/all_to_all | solution.py:204
  87.6 5.0 %all_gather.15.qkv_ref = bf16[1024,384]{1,0:T(8,128)(2,1)S(1)} all-gather(bf16[512,384]{1,0:T(8,128)(2,1)S(1)} %bitcast.11), channel_id=1, replica_groups=mesh['xl'=2,'y'=4,'c'=2,'xh'=2,'z'=16] {'c'}, dimensions={0}, use_global_device_ids=true | all-gather | bytes 1179648 | tf_op jit(solution)/shard_map/all_gather | solution.py:205
  92.6 0.0 copy-done.1
  92.6 0.0 copy-done.2
  92.6 1.4 %shard_map.51 = bf16[4,64,128]{2,1,0:T(8,128)(2,1)S(1)} custom-call(s32[3,16]{1,0:T(4,128)S(1)} %copy-done.1, s32[3,4]{1,0:T(4,128)S(1)} %copy-done.2, bf16[1024,384]{1,0:T(8,128)(2,1)S(1)} %all_gather.15.qkv_ref), custom_call_target="tpu_custom_call" | custom-call | flops 200000000 | bytes 1000000 | tf_op jit(solution)/shard_map/pallas_call | solution.py:207
  94.0 6.8 %all_to_all.22 = bf16[4,64,128]{2,1,0:T(8,128)(2,1)S(1)} all-to-all(bf16[4,64,128]{2,1,0:T(8,128)(2,1)S(1)} %shard_map.51), channel_id=1, replica_groups=mesh['xl'=2,'y'=4,'c'=2,'xh'=2,'z'=16] {'y'}, dimensions={0} | all-to-all | bytes 131072 | tf_op jit(solution)/shard_map/all_to_all | solution.py:215
  100.9 0.6 slice_bitcast_fusion
  (1 shorter events, 0.0 us)
Async XLA Ops:
  12.7 0.9 copy-start
  15.0 38.1 %all-to-all-start = ((bf16[8,320,384]{2,1,0:T(8,128)(2,1)}), bf16[8,320,384]{2,1,0:T(8,128)(2,1)S(1)}, u32[]{:S(2)}, u32[]{:S(2)}) async-start(bf16[8,320,384]{2,1,0:T(8,128)(2,1)} %shard_map.46), calls=%async_computation | async-start | bytes 3932160 | tf_op jit(solution)/shard_map/all_to_all | solution.py:178
  54.4 8.8 %collective-permute-start = (f32[192,768]{1,0:T(8,128)S(1)}, f32[192,768]{1,0:T(8,128)S(1)}, u32[]{:S(2)}, u32[]{:S(2)}) collective-permute-start(f32[192,768]{1,0:T(8,128)S(1)} %get-tuple-element.12), channel_id=1, source_target_pairs={{0,32},{32,0},{1,33},{33,1},{2,34},{34,2},{3,35},{35,3},{4,36},{36... | collective-permute-start | bytes 1769480 | tf_op jit(solution)/shard_map/ppermute | solution.py:196
  63.3 29.3 %copy-start.1 = (s32[3,16]{1,0:T(4,128)S(1)}, s32[3,16]{1,0:T(4,128)}, u32[]{:S(2)}) copy-start(s32[3,16]{1,0:T(4,128)} %destination_ref.1) | copy-start | bytes 580
  63.3 29.3 %copy-start.2 = (s32[3,4]{1,0:T(4,128)S(1)}, s32[3,4]{1,0:T(4,128)}, u32[]{:S(2)}) copy-start(s32[3,4]{1,0:T(4,128)} %lengths_ref.1) | copy-start | bytes 148

commit v5 on v4

--- a/solution.py
+++ b/solution.py
@@ -91,7 +91,7 @@
     return (at & HALF) + ((at & (NZ - 1)) << 1) + ((at >> 4) & 1)
 
 
-def attend_kernel(destination_ref, lengths_ref, qkv_ref, out_ref, ordered_ref):
+def mask_kernel(destination_ref, lengths_ref, bias_ref, start_ref):
     xl, y_own, c = (lax.axis_index(a) for a in ("xl", "y", "c"))
     pack = jnp.minimum(y_own, NPACK - 1)
     ends = []
@@ -115,25 +115,28 @@
         key_block = jnp.where((lane >> 6) == slot, destination_ref[pack, j], key_block)
     key_ids = segment(key_block * BLK + row_of(lane))
 
-    queries = []
     for y in range(4):
         block = xl * 8 + y * 2 + c
         start = 0
         for j in range(NBLK):
             start = jnp.where(destination_ref[pack, j] == block, slots[j] * BLK, start)
-        start = pl.multiple_of(start, BLK)
-        queries.append(qkv_ref[pl.ds(start, BLK), 0:HD])
-    query = jnp.concatenate(queries, axis=0)
+        start_ref[y] = start
     row = lax.broadcasted_iota(jnp.int32, (4 * BLK, 1), 0)
     query_ids = segment((xl * 8 + c) * BLK + (row >> 6) * (2 * BLK) + row_of(row))
-
+    bias_ref[...] = jnp.where(query_ids == key_ids, 0.0, -jnp.inf)
+
+
+def attend_kernel(start_ref, bias_ref, qkv_ref, out_ref, ordered_ref):
+    query = jnp.concatenate(
+        [qkv_ref[pl.ds(pl.multiple_of(start_ref[y], BLK), BLK), 0:HD] for y in range(4)], axis=0
+    )
     scores = lax.dot_general(
         query,
         qkv_ref[:, HD : 2 * HD],
         (((1,), (1,)), ((), ())),
         preferred_element_type=jnp.float32,
     ) * (HD**-0.5)
-    scores = jnp.where(query_ids == key_ids, scores, -jnp.inf)
+    scores = scores + bias_ref[...]
     weights = jnp.exp(scores - jnp.max(scores, axis=-1, keepdims=True))
     weights = (weights * (1.0 / jnp.sum(weights, axis=-1, keepdims=True))).astype(jnp.bfloat16)
     attended = jnp.dot(weights, qkv_ref[:, 2 * HD : 3 * HD], preferred_element_type=jnp.float32)
@@ -204,13 +207,23 @@
     blocks = lax.all_to_all(spread, ("xl", "y"), 0, 0, tiled=True)
     blocks = lax.all_gather(blocks.reshape(8 * BLK, QKV), "c", axis=0, tiled=True)
 
+    bias, starts = call(
+        mask_kernel,
+        (
+            jax.ShapeDtypeStruct((4 * BLK, NBLK * BLK), jnp.float32),
+            jax.ShapeDtypeStruct((4,), jnp.int32),
+        ),
+        [whole(pltpu.SMEM)] * 2,
+        cost=(10**6, 10**6, 0),
+        out_specs=(whole(), whole(pltpu.SMEM)),
+    )(destination, image_lengths)
     attended = call(
         attend_kernel,
         jax.ShapeDtypeStruct((4, BLK, HD), half_type),
-        [whole(pltpu.SMEM)] * 2 + [whole()],
+        [whole(pltpu.SMEM), whole(), whole()],
         [pltpu.VMEM((4 * BLK + 8, HD), jnp.float32)],
         cost=(2 * 10**8, 10**6, 3 * 10**5),
-    )(destination, image_lengths, blocks)
+    )(starts, bias, blocks)
 
     home = lax.all_to_all(attended, "y", 0, 0, tiled=True)
     return home[:NPACK].reshape(NPACK, BLK, 1, HD)

time: 102 us -> 102 us (level)
  blocking collectives: 83 us -> 72.2 us
  waiting for transfers between devices: 1.61 us -> 6.89 us
  starting transfers between devices: 10.8 us -> 14.7 us
  Pallas kernels: 4.45 us -> 6.4 us
    all_to_all x1 -> x0, blocking collectives: 10.7 us -> none  [shards(): blocks = lax.all_to_all(spread, ('xl', 'y'), 0, 0, tiled=True)]
    all_to_all x0 -> x1, waiting for transfers between devices: none -> 5.28 us  [shards(): blocks = lax.all_to_all(spread, ('xl', 'y'), 0, 0, tiled=True)]
    all_to_all x0 -> x1, starting transfers between devices: none -> 3.97 us  [shards(): blocks = lax.all_to_all(spread, ('xl', 'y'), 0, 0, tiled=True)]
    pallas_call x0 -> x1, Pallas kernels: none -> 1.31 us  [shards(): call(mask_kernel, (jax.ShapeDtypeStruct((4 * BLK, NBLK * BLK), jnp.float3...]
  transfers between devices with their start and end apart: 2 -> 3, of which waited for: 1 -> 2; matrix products, arithmetic and copies ran while one was open for 0% -> 0% of each run, Pallas kernels for 0% -> 1%
where the time goes in v5:
time: 102 us
  blocking collectives  72.2 us (71%)
  starting transfers between devices  14.7 us (14%)
  waiting for transfers between devices  6.89 us (7%)
  Pallas kernels  6.4 us (6%)
  local copies, waits for them, and re-layouts  1.58 us (2%)
    all_gather x1, blocking collectives, shards(): rows = lax.all_gather(rows, 'z', axis=0, tiled=True)  34.3 us
    all_to_all x1, blocking collectives, shards(): parts = lax.all_to_all(spread, ('xl', 'xh'), 0, 0, tiled=True)  13.5 us
    all_gather x1, blocking collectives, shards(): near = lax.all_gather(patches, ('xl', 'c'), axis=0)  12.5 us
    ppermute x1, starting transfers between devices, shards(): got = lax.ppermute(give, 'c', [(0, 1), (1, 0)])  7.17 us
    all_to_all x1, blocking collectives, shards(): home = lax.all_to_all(attended, 'y', 0, 0, tiled=True)  6.84 us
    all_to_all x1, waiting for transfers between devices, shards(): blocks = lax.all_to_all(spread, ('xl', 'y'), 0, 0, tiled=True)  5.28 us
    all_gather x1, blocking collectives, shards(): lax.all_gather(blocks.reshape(8 * BLK, QKV), 'c', axis=0, tiled=True)  5.13 us
    all_to_all x1, starting transfers between devices, shards(): blocks = lax.all_to_all(spread, ('xl', 'y'), 0, 0, tiled=True)  3.97 us
  transfers between devices with their start and end apart: 3, of which 2 were waited for; matrix products, arithmetic and copies ran while one was open for 0% of the time, Pallas kernels for 1%

profile of v5, /device:TPU:1, one launch (start us, length us, event | category | flops | bytes accessed | tf_op | source)
XLA Modules:
  0.0 101.9 jit_solution(13380788153178251568)
XLA Ops:
  0.0 0.0 copy-start
  0.0 0.9 copy-done
  0.9 1.4 %shard_map.47 = bf16[8,320,384]{2,1,0:T(8,128)(2,1)} custom-call(bf16[320,384]{1,0:T(8,128)(2,1)S(1)} %bitcast.10), custom_call_target="tpu_custom_call" | custom-call | bytes 1000000 | tf_op jit(solution)/shard_map/pallas_call | solution.py:172
  2.3 0.0 copy-done.3
  2.3 12.5 %all-gather = bf16[12,2,5120]{2,1,0:T(2,128)(2,1)S(1)} all-gather(bf16[3,2,5120]{2,1,0:T(2,128)(2,1)S(1)} %copy-done.3), channel_id=2, replica_groups=mesh['xl'=2,'y'=4,'c'=2,'xh'=2,'z'=16] {'xl','c'}, dimensions={0}, use_global_device_ids=true | all-gather | bytes 307200 | tf_op jit(solution)/shard_map/all_gather | solution.py:179
  14.8 3.6 %all-to-all-start = ((bf16[8,320,384]{2,1,0:T(8,128)(2,1)}), bf16[8,320,384]{2,1,0:T(8,128)(2,1)S(1)}, u32[]{:S(2)}, u32[]{:S(2)}) async-start(bf16[8,320,384]{2,1,0:T(8,128)(2,1)} %shard_map.47), calls=%async_computation | async-start | bytes 3932160 | tf_op jit(solution)/shard_map/all_to_all | solution.py:181
  18.4 0.2 shard_map.48
  18.6 34.3 %all_gather.14.x_ref = bf16[384,1280]{1,0:T(8,128)(2,1)S(1)} all-gather(bf16[24,1280]{1,0:T(8,128)(2,1)S(1)} %shard_map.48), channel_id=1, replica_groups=mesh['xl'=2,'y'=4,'c'=2,'xh'=2,'z'=16] {'z'}, dimensions={0}, use_global_device_ids=true | all-gather | bytes 1044480 | tf_op jit(solution)/shard_map/all_gather | solution.py:186
  52.9 0.0 all-to-all-done
  52.9 1.3 %shard_map.49 = (f32[192,768]{1,0:T(8,128)S(1)}, f32[192,768]{1,0:T(8,128)S(1)}) custom-call(bf16[384,1280]{1,0:T(8,128)(2,1)S(1)} %all_gather.14.x_ref, bf16[4,2,320,384]{3,2,1,0:T(8,128)(2,1)S(1)} %bitcast.8), custom_call_target="tpu_custom_call" | custom-call | flops 1000000000 | bytes 4000000 | tf_op jit(solution)/shard_map/pallas_call | solution.py:188
  54.2 7.2 %collective-permute-start = (f32[192,768]{1,0:T(8,128)S(1)}, f32[192,768]{1,0:T(8,128)S(1)}, u32[]{:S(2)}, u32[]{:S(2)}) collective-permute-start(f32[192,768]{1,0:T(8,128)S(1)} %get-tuple-element.16), channel_id=1, source_target_pairs={{0,32},{32,0},{1,33},{33,1},{2,34},{34,2},{3,35},{35,3},{4,36},{36... | collective-permute-start | bytes 1769480 | tf_op jit(solution)/shard_map/ppermute | solution.py:199
  61.4 1.6 %collective-permute-done.got_ref = f32[192,768]{1,0:T(8,128)S(1)} collective-permute-done((f32[192,768]{1,0:T(8,128)S(1)}, f32[192,768]{1,0:T(8,128)S(1)}, u32[]{:S(2)}, u32[]{:S(2)}) %collective-permute-start) | collective-permute-done | bytes 589856 | tf_op jit(solution)/shard_map/ppermute | solution.py:199
  63.0 0.1 shard_map.50
  63.1 13.5 %all_to_all.20.parts_ref = f32[4,96,384]{2,1,0:T(8,128)S(1)} all-to-all(f32[4,96,384]{2,1,0:T(8,128)S(1)} %shard_map.50), channel_id=1, replica_groups=mesh['xl'=2,'y'=4,'c'=2,'xh'=2,'z'=16] {'xl','xh'}, dimensions={0} | all-to-all | bytes 1179648 | tf_op jit(solution)/shard_map/all_to_all | solution.py:205
  76.6 0.8 shard_map.51
  77.4 4.0 %all-to-all-start.2 = ((bf16[8,64,384]{2,1,0:T(8,128)(2,1)}), bf16[8,64,384]{2,1,0:T(8,128)(2,1)S(1)}, u32[]{:S(2)}, u32[]{:S(2)}) async-start(bf16[8,64,384]{2,1,0:T(8,128)(2,1)} %shard_map.51), calls=%async_computation.2 | async-start | bytes 786432 | tf_op jit(solution)/shard_map/all_to_all | solution.py:207
  81.3 0.0 copy-done.1
  81.3 0.0 copy-done.2
  81.3 1.3 %shard_map.46 = (f32[256,1024]{1,0:T(8,128)S(1)}, s32[4]{0:T(128)S(1)}) custom-call(s32[3,16]{1,0:T(4,128)S(1)} %copy-done.1, s32[3,4]{1,0:T(4,128)S(1)} %copy-done.2), custom_call_target="tpu_custom_call" | custom-call | flops 1000000 | bytes 1000000 | tf_op jit(solution)/shard_map/pallas_call | solution.py:210
  82.7 5.3 %all-to-all-done.2 = bf16[8,64,384]{2,1,0:T(8,128)(2,1)S(1)} async-done(((bf16[8,64,384]{2,1,0:T(8,128)(2,1)}), bf16[8,64,384]{2,1,0:T(8,128)(2,1)S(1)}, u32[]{:S(2)}, u32[]{:S(2)}) %all-to-all-start.2) | async-done | bytes 393248 | tf_op jit(solution)/shard_map/all_to_all | solution.py:207
  87.9 5.1 %all_gather.15.qkv_ref = bf16[1024,384]{1,0:T(8,128)(2,1)S(1)} all-gather(bf16[512,384]{1,0:T(8,128)(2,1)S(1)} %bitcast.11), channel_id=1, replica_groups=mesh['xl'=2,'y'=4,'c'=2,'xh'=2,'z'=16] {'c'}, dimensions={0}, use_global_device_ids=true | all-gather | bytes 1179648 | tf_op jit(solution)/shard_map/all_gather | solution.py:208
  93.1 1.3 %shard_map.52 = bf16[4,64,128]{2,1,0:T(8,128)(2,1)S(1)} custom-call(s32[4]{0:T(128)S(1)} %get-tuple-element.11.start_ref, f32[256,1024]{1,0:T(8,128)S(1)} %get-tuple-element.12.bias_ref, bf16[1024,384]{1,0:T(8,128)(2,1)S(1)} %all_gather.15.qkv_ref), custom_call_target="tpu_custom_call" | custom-call | flops 200000000 | bytes 1000000 | tf_op jit(solution)/shard_map/pallas_call | solution.py:220
  94.4 6.8 %all_to_all.21 = bf16[4,64,128]{2,1,0:T(8,128)(2,1)S(1)} all-to-all(bf16[4,64,128]{2,1,0:T(8,128)(2,1)S(1)} %shard_map.52), channel_id=1, replica_groups=mesh['xl'=2,'y'=4,'c'=2,'xh'=2,'z'=16] {'y'}, dimensions={0} | all-to-all | bytes 131072 | tf_op jit(solution)/shard_map/all_to_all | solution.py:228
  101.3 0.6 slice_bitcast_fusion
  (3 shorter events, 0.0 us)
Async XLA Ops:
  0.0 0.9 copy-start
  0.9 1.4 %copy-start.3 = (bf16[3,2,5120]{2,1,0:T(2,128)(2,1)S(1)}, bf16[3,2,5120]{2,1,0:T(2,128)(2,1)}, u32[]{:S(2)}) copy-start(bf16[3,2,5120]{2,1,0:T(2,128)(2,1)} %param.4) | copy-start | bytes 184324
  14.8 38.1 %all-to-all-start = ((bf16[8,320,384]{2,1,0:T(8,128)(2,1)}), bf16[8,320,384]{2,1,0:T(8,128)(2,1)S(1)}, u32[]{:S(2)}, u32[]{:S(2)}) async-start(bf16[8,320,384]{2,1,0:T(8,128)(2,1)} %shard_map.47), calls=%async_computation | async-start | bytes 3932160 | tf_op jit(solution)/shard_map/all_to_all | solution.py:181
  54.2 8.8 %collective-permute-start = (f32[192,768]{1,0:T(8,128)S(1)}, f32[192,768]{1,0:T(8,128)S(1)}, u32[]{:S(2)}, u32[]{:S(2)}) collective-permute-start(f32[192,768]{1,0:T(8,128)S(1)} %get-tuple-element.16), channel_id=1, source_target_pairs={{0,32},{32,0},{1,33},{33,1},{2,34},{34,2},{3,35},{35,3},{4,36},{36... | collective-permute-start | bytes 1769480 | tf_op jit(solution)/shard_map/ppermute | solution.py:199
  63.0 18.4 %copy-start.1 = (s32[3,16]{1,0:T(4,128)S(1)}, s32[3,16]{1,0:T(4,128)}, u32[]{:S(2)}) copy-start(s32[3,16]{1,0:T(4,128)} %destination_ref.1) | copy-start | bytes 580
  63.0 18.4 %copy-start.2 = (s32[3,4]{1,0:T(4,128)S(1)}, s32[3,4]{1,0:T(4,128)}, u32[]{:S(2)}) copy-start(s32[3,4]{1,0:T(4,128)} %lengths_ref.1) | copy-start | bytes 148
  77.4 10.6 %all-to-all-start.2 = ((bf16[8,64,384]{2,1,0:T(8,128)(2,1)}), bf16[8,64,384]{2,1,0:T(8,128)(2,1)S(1)}, u32[]{:S(2)}, u32[]{:S(2)}) async-start(bf16[8,64,384]{2,1,0:T(8,128)(2,1)} %shard_map.51), calls=%async_computation.2 | async-start | bytes 786432 | tf_op jit(solution)/shard_map/all_to_all | solution.py:207

commit v6 on v4

--- a/solution.py
+++ b/solution.py
@@ -48,22 +48,20 @@
 
 def project_kernel(x_ref, w_ref, keep_ref, give_ref, product_ref):
     own = lax.axis_index("c")
-    for head in range(2):
-        product = jnp.dot(
-            x_ref[...], w_ref[:, head].reshape(KSET, QKV), preferred_element_type=jnp.float32
-        )
-        for k in range(3):
-            product_ref[k, : 4 * LOCAL * NZ] = product[:, k * HD : (k + 1) * HD]
-            columns = slice(head * QKV + k * HD, head * QKV + (k + 1) * HD)
-            for p in range(NPACK):
-                for xl in range(2):
-                    for i in range(2):
-                        at = p * BLK + xl * HALF + i * NZ
-                        first = xl * 2 * LOCAL + p * 2 + i
-                        mine = product_ref[k, pl.ds(first + own * LOCAL, NZ, stride=4 * LOCAL), :]
-                        theirs = product_ref[k, pl.ds(first + (1 - own) * LOCAL, NZ, stride=4 * LOCAL), :]
-                        keep_ref[at : at + NZ, columns] = mine
-                        give_ref[at : at + NZ, columns] = theirs
+    both = jnp.concatenate([w_ref[:, head].reshape(KSET, QKV) for head in range(2)], axis=1)
+    product = jnp.dot(x_ref[...], both, preferred_element_type=jnp.float32)
+    for k in range(6):
+        product_ref[k, : 4 * LOCAL * NZ] = product[:, k * HD : (k + 1) * HD]
+        columns = slice(k * HD, (k + 1) * HD)
+        for p in range(NPACK):
+            for xl in range(2):
+                for i in range(2):
+                    at = p * BLK + xl * HALF + i * NZ
+                    first = xl * 2 * LOCAL + p * 2 + i
+                    mine = product_ref[k, pl.ds(first + own * LOCAL, NZ, stride=4 * LOCAL), :]
+                    theirs = product_ref[k, pl.ds(first + (1 - own) * LOCAL, NZ, stride=4 * LOCAL), :]
+                    keep_ref[at : at + NZ, columns] = mine
+                    give_ref[at : at + NZ, columns] = theirs
 
 
 def pair_kernel(keep_ref, got_ref, out_ref):
@@ -189,7 +187,7 @@
             jax.ShapeDtypeStruct((ROWS, 2 * QKV), jnp.float32),
         ),
         [whole(), whole()],
-        [pltpu.VMEM((3, 4 * LOCAL * (NZ + 1), HD), jnp.float32)],
+        [pltpu.VMEM((6, 4 * LOCAL * (NZ + 1), HD), jnp.float32)],
         cost=(10**9, 4 * 10**6, 0),
     )(rows, weight_set.reshape(4, 2, PIECE, QKV))
 

time: 102 us -> 102 us (level)
  no operation moved by 1% of the time
where the time goes in v6:
time: 102 us; the launch traced here: 101 us
  blocking collectives  83 us (81%)
  starting transfers between devices  10.8 us (11%)
  Pallas kernels  4.23 us (4%)
  waiting for transfers between devices  1.61 us (2%)
  local copies, waits for them, and re-layouts  1.58 us (2%)
    all_gather x1, blocking collectives, shards(): rows = lax.all_gather(rows, 'z', axis=0, tiled=True)  34.3 us
    all_to_all x1, blocking collectives, shards(): parts = lax.all_to_all(spread, ('xl', 'xh'), 0, 0, tiled=True)  13.5 us
    all_gather x1, blocking collectives, shards(): near = lax.all_gather(patches, ('xl', 'c'), axis=0)  12.7 us
    all_to_all x1, blocking collectives, shards(): blocks = lax.all_to_all(spread, ('xl', 'y'), 0, 0, tiled=True)  10.7 us
    ppermute x1, starting transfers between devices, shards(): got = lax.ppermute(give, 'c', [(0, 1), (1, 0)])  7.17 us
    all_to_all x1, blocking collectives, shards(): home = lax.all_to_all(attended, 'y', 0, 0, tiled=True)  6.84 us
    all_gather x1, blocking collectives, shards(): lax.all_gather(blocks.reshape(8 * BLK, QKV), 'c', axis=0, tiled=True)  5 us
    all_to_all x1, starting transfers between devices, shards(): weight_set = lax.all_to_all(slots, ('y', 'xh'), 0, 0, tiled=True)  3.61 us
  transfers between devices with their start and end apart: 2, of which 1 were waited for; matrix products, arithmetic and copies ran while one was open for 0% of the time, Pallas kernels for 0%

profile of v6, /device:TPU:1, one launch (start us, length us, event | category | flops | bytes accessed | tf_op | source)
XLA Modules:
  0.0 101.3 jit_solution(8058217401943335365)
XLA Ops:
  0.0 12.7 %all-gather = bf16[12,2,5120]{2,1,0:T(2,128)(2,1)S(1)} all-gather(bf16[3,2,5120]{2,1,0:T(2,128)(2,1)} %param.4), channel_id=2, replica_groups=mesh['xl'=2,'y'=4,'c'=2,'xh'=2,'z'=16] {'xl','c'}, dimensions={0}, use_global_device_ids=true | all-gather | bytes 307200 | tf_op jit(solution)/shard_map/all_gather | solution.py:174
  12.7 0.0 copy-start
  12.7 0.9 copy-done
  13.6 1.4 %shard_map.46 = bf16[8,320,384]{2,1,0:T(8,128)(2,1)} custom-call(bf16[320,384]{1,0:T(8,128)(2,1)S(1)} %bitcast.10), custom_call_target="tpu_custom_call" | custom-call | bytes 1000000 | tf_op jit(solution)/shard_map/pallas_call | solution.py:167
  15.0 3.6 %all-to-all-start = ((bf16[8,320,384]{2,1,0:T(8,128)(2,1)}), bf16[8,320,384]{2,1,0:T(8,128)(2,1)S(1)}, u32[]{:S(2)}, u32[]{:S(2)}) async-start(bf16[8,320,384]{2,1,0:T(8,128)(2,1)} %shard_map.46), calls=%async_computation | async-start | bytes 3932160 | tf_op jit(solution)/shard_map/all_to_all | solution.py:176
  18.6 0.2 shard_map.47
  18.8 34.3 %all_gather.14.x_ref = bf16[384,1280]{1,0:T(8,128)(2,1)S(1)} all-gather(bf16[24,1280]{1,0:T(8,128)(2,1)S(1)} %shard_map.47), channel_id=1, replica_groups=mesh['xl'=2,'y'=4,'c'=2,'xh'=2,'z'=16] {'z'}, dimensions={0}, use_global_device_ids=true | all-gather | bytes 1044480 | tf_op jit(solution)/shard_map/all_gather | solution.py:181
  53.1 0.0 all-to-all-done
  53.1 1.1 %shard_map.48 = (f32[192,768]{1,0:T(8,128)S(1)}, f32[192,768]{1,0:T(8,128)S(1)}) custom-call(bf16[384,1280]{1,0:T(8,128)(2,1)S(1)} %all_gather.14.x_ref, bf16[4,2,320,384]{3,2,1,0:T(8,128)(2,1)S(1)} %bitcast.8), custom_call_target="tpu_custom_call" | custom-call | flops 1000000000 | bytes 4000000 | tf_op jit(solution)/shard_map/pallas_call | solution.py:183
  54.2 7.2 %collective-permute-start = (f32[192,768]{1,0:T(8,128)S(1)}, f32[192,768]{1,0:T(8,128)S(1)}, u32[]{:S(2)}, u32[]{:S(2)}) collective-permute-start(f32[192,768]{1,0:T(8,128)S(1)} %get-tuple-element.12), channel_id=1, source_target_pairs={{0,32},{32,0},{1,33},{33,1},{2,34},{34,2},{3,35},{35,3},{4,36},{36... | collective-permute-start | bytes 1769480 | tf_op jit(solution)/shard_map/ppermute | solution.py:194
  61.4 1.6 %collective-permute-done.got_ref = f32[192,768]{1,0:T(8,128)S(1)} collective-permute-done((f32[192,768]{1,0:T(8,128)S(1)}, f32[192,768]{1,0:T(8,128)S(1)}, u32[]{:S(2)}, u32[]{:S(2)}) %collective-permute-start) | collective-permute-done | bytes 589856 | tf_op jit(solution)/shard_map/ppermute | solution.py:194
  63.0 0.1 shard_map.49
  63.0 0.0 copy-start.1
  63.1 0.0 copy-start.2
  63.1 13.5 %all_to_all.20.parts_ref = f32[4,96,384]{2,1,0:T(8,128)S(1)} all-to-all(f32[4,96,384]{2,1,0:T(8,128)S(1)} %shard_map.49), channel_id=1, replica_groups=mesh['xl'=2,'y'=4,'c'=2,'xh'=2,'z'=16] {'xl','xh'}, dimensions={0} | all-to-all | bytes 1179648 | tf_op jit(solution)/shard_map/all_to_all | solution.py:200
  76.6 10.7 %all_to_all.21 = bf16[8,64,384]{2,1,0:T(8,128)(2,1)S(1)} all-to-all(bf16[8,64,384]{2,1,0:T(8,128)(2,1)S(1)} %shard_map.50), channel_id=1, replica_groups=mesh['xl'=2,'y'=4,'c'=2,'xh'=2,'z'=16] {'xl','y'}, dimensions={0} | all-to-all | bytes 786432 | tf_op jit(solution)/shard_map/all_to_all | solution.py:202
  87.4 5.0 %all_gather.15.qkv_ref = bf16[1024,384]{1,0:T(8,128)(2,1)S(1)} all-gather(bf16[512,384]{1,0:T(8,128)(2,1)S(1)} %bitcast.11), channel_id=1, replica_groups=mesh['xl'=2,'y'=4,'c'=2,'xh'=2,'z'=16] {'c'}, dimensions={0}, use_global_device_ids=true | all-gather | bytes 1179648 | tf_op jit(solution)/shard_map/all_gather | solution.py:203
  92.4 0.0 copy-done.1
  92.4 0.0 copy-done.2
  92.4 1.4 %shard_map.51 = bf16[4,64,128]{2,1,0:T(8,128)(2,1)S(1)} custom-call(s32[3,16]{1,0:T(4,128)S(1)} %copy-done.1, s32[3,4]{1,0:T(4,128)S(1)} %copy-done.2, bf16[1024,384]{1,0:T(8,128)(2,1)S(1)} %all_gather.15.qkv_ref), custom_call_target="tpu_custom_call" | custom-call | flops 200000000 | bytes 1000000 | tf_op jit(solution)/shard_map/pallas_call | solution.py:205
  93.8 6.8 %all_to_all.22 = bf16[4,64,128]{2,1,0:T(8,128)(2,1)S(1)} all-to-all(bf16[4,64,128]{2,1,0:T(8,128)(2,1)S(1)} %shard_map.51), channel_id=1, replica_groups=mesh['xl'=2,'y'=4,'c'=2,'xh'=2,'z'=16] {'y'}, dimensions={0} | all-to-all | bytes 131072 | tf_op jit(solution)/shard_map/all_to_all | solution.py:213
  100.7 0.6 slice_bitcast_fusion
  (1 shorter events, 0.0 us)
Async XLA Ops:
  12.7 0.9 copy-start
  15.0 38.1 %all-to-all-start = ((bf16[8,320,384]{2,1,0:T(8,128)(2,1)}), bf16[8,320,384]{2,1,0:T(8,128)(2,1)S(1)}, u32[]{:S(2)}, u32[]{:S(2)}) async-start(bf16[8,320,384]{2,1,0:T(8,128)(2,1)} %shard_map.46), calls=%async_computation | async-start | bytes 3932160 | tf_op jit(solution)/shard_map/all_to_all | solution.py:176
  54.2 8.8 %collective-permute-start = (f32[192,768]{1,0:T(8,128)S(1)}, f32[192,768]{1,0:T(8,128)S(1)}, u32[]{:S(2)}, u32[]{:S(2)}) collective-permute-start(f32[192,768]{1,0:T(8,128)S(1)} %get-tuple-element.12), channel_id=1, source_target_pairs={{0,32},{32,0},{1,33},{33,1},{2,34},{34,2},{3,35},{35,3},{4,36},{36... | collective-permute-start | bytes 1769480 | tf_op jit(solution)/shard_map/ppermute | solution.py:194
  63.0 29.3 %copy-start.1 = (s32[3,16]{1,0:T(4,128)S(1)}, s32[3,16]{1,0:T(4,128)}, u32[]{:S(2)}) copy-start(s32[3,16]{1,0:T(4,128)} %destination_ref.1) | copy-start | bytes 580
  63.1 29.3 %copy-start.2 = (s32[3,4]{1,0:T(4,128)S(1)}, s32[3,4]{1,0:T(4,128)}, u32[]{:S(2)}) copy-start(s32[3,4]{1,0:T(4,128)} %lengths_ref.1) | copy-start | bytes 148
